TPU v7x, 128 devices: a whole 4x4x4 slice. The times are simulated.
128 devices in a mesh: row: 8 (over y, core), col: 16 (over x, z).
Axes of the slice: x: 4, y: 4, z: 4, core: 2. Of those that a mesh axis runs over, the one named last changes fastest.
Arguments:
- temp_thermal: float32 [16, 524288], P(None, ('row', 'col')), may hold values from -6 to 6
- send_index: int32 [128, 4096], P(('row', 'col')), may hold values from 0 to 4095
- interp_slot: int32 [4, 557056], P(None, ('row', 'col')), may hold values from 0 to 4095
- interp_weight: float32 [4, 557056], P(None, ('row', 'col')), may hold values from 0.1 to 1
- disp: bfloat16 [3, 16, 557056], P(None, None, ('row', 'col')), may hold values from -6 to 6
- expansion: float32 [3, 557056], P(None, ('row', 'col')), may hold values from -6 to 6
- tangent: bfloat16 [96, 96, 16384], P(None, None, ('row', 'col')), may hold values from -0.625 to 0.625
- connect: int32 [32, 16384], P(None, ('row', 'col')), may hold values from 0 to 4351
- recv_lower: int32 [16384], P(('row', 'col')), may hold values from 0 to 4095
- recv_upper: int32 [16384], P(('row', 'col')), may hold values from 0 to 4095
Outputs:
- residual: float32 [3, 16, 524288], P(None, None, ('row', 'col'))
Inputs may be any that keep to these rules, and one draw needn't show every extreme that they name: `send_index`: local thermal node indices of the sending partition. `interp_slot`: slots of the subdomain's received thermal values. `connect`: subdomain-local node copies; below 4096 owned, then 128 lower ghosts, then 128 upper ghosts. `recv_lower`: owned nodes of the receiving subdomain. `recv_upper`: owned nodes of the receiving subdomain.
All inputs are finite; a program needn't handle non-finite values.
Results may differ from a plain program's by a relative error of at most 0.0029.
Values sent between devices are 32-bit elements; how exact they have to be, the bound alone decides.
No kernel may reach another device: no remote copies, remote signals or barrier semaphores. Data moves between devices by JAX's collectives and lax.ppermute only.
A program may use at most 64 MiB of HBM per device.

v0:
```python
import functools

import jax
import jax.numpy as jnp
from jax import lax
from jax.experimental import pallas as pl
from jax.experimental.pallas import tpu as pltpu
from jax.sharding import PartitionSpec as P

F32 = jnp.float32
BF16 = jnp.bfloat16
I32 = jnp.int32
LANES = 128
WIDE = 256
AXES = ("row", "col")


def call(body, outs, scratch=()):
    return pl.pallas_call(
        body,
        out_shape=outs,
        scratch_shapes=scratch,
        compiler_params=pltpu.CompilerParams(vmem_limit_bytes=56 * 2**20),
    )


def split(x):
    high = x.astype(BF16)
    return high, (x - high.astype(F32)).astype(BF16)


def one_hot(low, iota):
    return jnp.where(iota == low.astype(F32).astype(BF16), jnp.ones((), BF16), jnp.zeros((), BF16))


def iota_of(columns):
    return lax.broadcasted_iota(I32, (WIDE, columns), 0).astype(F32).astype(BF16)


def choose(stacked, high, rows):
    out = stacked[0:rows]
    for h in range(1, stacked.shape[0] // rows):
        out = jnp.where(high == h, stacked[rows * h : rows * (h + 1)], out)
    return out


def swap_blocks(x):
    row = lax.broadcasted_iota(I32, x.shape, 0) >> 2
    col = lax.broadcasted_iota(I32, x.shape, 1) >> 5
    out = x
    for d in range(1, 4):
        moved = pltpu.roll(pltpu.roll(x, 16 - 4 * d, 0), 32 * d, 1)
        out = jnp.where(((col - row) & 3) == d, moved, out)
    return out


def fill_table(tab, read, blocks):
    for h in range(blocks):
        high, low = split(read(h))
        rows = high.shape[0]
        tab[h * rows : (h + 1) * rows, 0:WIDE] = high
        tab[h * rows : (h + 1) * rows, WIDE : 2 * WIDE] = low


def send_kernel(temp, index, out, tab):
    fill_table(tab, lambda h: temp[:, h * WIDE : (h + 1) * WIDE], temp.shape[1] // WIDE)
    iota = iota_of(WIDE)

    def body(j, _):
        idx = index[0:1, pl.ds(pl.multiple_of(j * WIDE, WIDE), WIDE)]
        hot = one_hot(idx & (WIDE - 1), iota)
        stacked = jnp.dot(tab[...], jnp.concatenate([hot, hot], 0), preferred_element_type=F32)
        got = choose(stacked, idx >> 8, 16)
        out[2 * j] = swap_blocks(got[:, 0:LANES])
        out[2 * j + 1] = swap_blocks(got[:, LANES:])
        return 0

    lax.fori_loop(0, index.shape[1] // WIDE, body, 0)


def main_kernel(arrived, slot, weight, disp, expansion, tangent, connect, prod, ghosts, tab, tab3, hot, vec, tf):
    extent = slot.shape[1]

    def table(h):
        return jnp.concatenate([swap_blocks(arrived[2 * h]), swap_blocks(arrived[2 * h + 1])], 1)

    fill_table(tab, table, arrived.shape[0] // 2)
    iota = iota_of(WIDE)

    def interpolate(j, _):
        js = pl.ds(pl.multiple_of(j * WIDE, WIDE), WIDE)
        temp = jnp.zeros((16, WIDE), F32)
        for c in range(4):
            idx = slot[pl.ds(c, 1), js]
            h2 = one_hot(idx & (WIDE - 1), iota)
            stacked = jnp.dot(tab[...], jnp.concatenate([h2, h2], 0), preferred_element_type=F32)
            temp = temp + weight[pl.ds(c, 1), js] * choose(stacked, idx >> 8, 16)
        strain = temp / jnp.sqrt(1.0 + temp * temp)
        for a in range(3):
            d = disp[16 * a : 16 * a + 16, js].astype(F32)
            s = (d - expansion[a : a + 1, js] * strain).astype(BF16)
            tab3[pl.ds(pl.multiple_of(j * 48 + a * 16, 16), 16), :] = s
        return 0

    lax.fori_loop(0, extent // WIDE, interpolate, 0)

    for p in range(16):
        idx = jnp.concatenate([connect[2 * p : 2 * p + 1, :], connect[2 * p + 1 : 2 * p + 2, :]], 1)
        h1 = one_hot(idx & (WIDE - 1), iota)
        hot[:, p * WIDE : (p + 1) * WIDE] = h1
        stacked = jnp.dot(tab3[...], h1, preferred_element_type=F32)
        got = choose(stacked, idx >> 8, 48)
        for a in range(3):
            vec[a * 32 + 2 * p] = got[16 * a : 16 * a + 16, 0:LANES]
            vec[a * 32 + 2 * p + 1] = got[16 * a : 16 * a + 16, LANES:]

    def widen(i, _):
        tf[pl.ds(pl.multiple_of(i * 96, 96), 96), :] = tangent[i].astype(F32)
        return 0

    lax.fori_loop(0, 96, widen, 0)
    group = 8

    def cluster(b, _):
        def inner(j8, sums):
            sums = list(sums)
            for jj in range(8):
                j = j8 * 8 + jj
                upper, lower = vec[j, 0:8, :], vec[j, 8:16, :]
                for i in range(group):
                    row = tf[pl.ds((b * group + i) * 96 + j, 1), :]
                    sums[2 * i] = sums[2 * i] + row * upper
                    sums[2 * i + 1] = sums[2 * i + 1] + row * lower
            return tuple(sums)

        sums = lax.fori_loop(0, 12, inner, tuple([jnp.zeros((8, LANES), F32)] * (2 * group)))
        a, m = b // 4, (b % 4) * group
        for i in range(group):
            cs = pl.ds(pl.multiple_of((m + i) * LANES, LANES), LANES)
            prod[pl.ds(pl.multiple_of(a * 16, 8), 8), cs] = sums[2 * i]
            prod[pl.ds(pl.multiple_of(a * 16 + 8, 8), 8), cs] = sums[2 * i + 1]
        return 0

    lax.fori_loop(0, 96 // group, cluster, 0)

    total = jnp.zeros((96, WIDE), F32)
    for p in range(16):
        idx = jnp.concatenate([connect[2 * p : 2 * p + 1, :], connect[2 * p + 1 : 2 * p + 2, :]], 1)
        x = jnp.where((idx >> 8) == 16, prod[:, p * WIDE : (p + 1) * WIDE], 0.0)
        total = total + lax.dot_general(
            jnp.concatenate(split(x), 0),
            hot[:, p * WIDE : (p + 1) * WIDE],
            (((1,), (1,)), ((), ())),
            preferred_element_type=F32,
        )
    ghosts[...] = total[0:48] + total[48:96]


def spread(values, high, hot_t, blocks):
    rows = []
    for part in split(values):
        wide = part.astype(F32)
        rows += [jnp.where(high == h, wide, 0.0).astype(BF16) for h in range(blocks)]
    both = lax.dot_general(
        jnp.concatenate(rows, 0), hot_t, (((1,), (1,)), ((), ())), preferred_element_type=F32
    )
    half = blocks * 48
    return both[0:half] + both[half:]


def owned_kernel(prod, connect, out, a_scr, hot):
    blocks = out.shape[1] // WIDE
    half = blocks * 48
    iota = iota_of(WIDE)
    for p in range(16):
        ks = slice(p * WIDE, (p + 1) * WIDE)
        idx = jnp.concatenate([connect[2 * p : 2 * p + 1, :], connect[2 * p + 1 : 2 * p + 2, :]], 1)
        hot[:, ks] = one_hot(idx & (WIDE - 1), iota)
        high, low = split(prod[:, ks])
        high, low = high.astype(F32), low.astype(F32)
        for h in range(blocks):
            mask = (idx >> 8) == h
            a_scr[h * 48 : (h + 1) * 48, ks] = jnp.where(mask, high, 0.0).astype(BF16)
            a_scr[half + h * 48 : half + (h + 1) * 48, ks] = jnp.where(mask, low, 0.0).astype(BF16)
    dims = (((1,), (1,)), ((), ()))
    total = lax.dot_general(a_scr[0:half], hot[...], dims, preferred_element_type=F32)
    total = total + lax.dot_general(a_scr[half:], hot[...], dims, preferred_element_type=F32)
    for h in range(blocks):
        out[:, h * WIDE : (h + 1) * WIDE] = total[48 * h : 48 * h + 48]


def ghost_kernel(own, from_lower, from_upper, lower, upper, out):
    blocks = out.shape[1] // WIDE
    idx = jnp.concatenate([lower[...], upper[...]], 1)
    hot = one_hot(idx & (WIDE - 1), iota_of(WIDE))
    total = spread(jnp.concatenate([from_lower[...], from_upper[...]], 1), idx >> 8, hot, blocks)
    for h in range(blocks):
        hs = slice(h * WIDE, (h + 1) * WIDE)
        out[:, hs] = own[:, hs] + total[48 * h : 48 * h + 48]


def neighbour(block, distance):
    devices = range(lax.axis_size("col"))
    route = [(i - distance, i) for i in devices if i - distance in devices]
    return lax.ppermute(block, "col", route)


def shards(temp_thermal, send_index, interp_slot, interp_weight, disp, expansion, tangent, connect, recv_lower, recv_upper):
    shape = jax.ShapeDtypeStruct
    packed = call(
        send_kernel, shape((32, 16, LANES), F32), [pltpu.VMEM((256, 2 * WIDE), BF16)]
    )(temp_thermal, send_index)
    arrived = lax.all_to_all(packed.reshape(128, 4, LANES), AXES, split_axis=0, concat_axis=0, tiled=True)
    arrived = arrived.reshape(32, 16, LANES)
    prod, ghosts = call(
        main_kernel,
        (shape((48, 4096), F32), shape((48, WIDE), F32)),
        [
            pltpu.VMEM((256, 2 * WIDE), BF16),
            pltpu.VMEM((17 * 48, WIDE), BF16),
            pltpu.VMEM((WIDE, 4096), BF16),
            pltpu.VMEM((96, 16, LANES), F32),
            pltpu.VMEM((96 * 96, LANES), F32),
        ],
    )(arrived, interp_slot, interp_weight, disp.reshape(48, -1), expansion, tangent, connect)
    from_lower = neighbour(ghosts[:, LANES:], 1)
    from_upper = neighbour(ghosts[:, :LANES], -1)
    own = call(
        owned_kernel,
        shape((48, 4096), F32),
        [pltpu.VMEM((2 * 16 * 48, 4096), BF16), pltpu.VMEM((WIDE, 4096), BF16)],
    )(prod, connect)
    result = call(ghost_kernel, shape((48, 4096), F32))(
        own, from_lower, from_upper, recv_lower.reshape(1, LANES), recv_upper.reshape(1, LANES)
    )
    return result.reshape(3, 16, 4096)


def solution(mesh):
    in_specs = (
        P(None, AXES),
        P(AXES, None),
        P(None, AXES),
        P(None, AXES),
        P(None, None, AXES),
        P(None, AXES),
        P(None, None, AXES),
        P(None, AXES),
        P(AXES),
        P(AXES),
    )
    out_specs = P(None, None, AXES)
    return jax.shard_map(shards, mesh=mesh, in_specs=in_specs, out_specs=out_specs, check_vma=False)
```

profile of v0, /device:TPU:1, one launch (start us, length us, event | category | flops | bytes accessed | tf_op | source)
XLA Modules:
  0.0 65.6 jit_solution(2558702691210361994)
XLA Ops:
  0.0 6.7 %shard_map.100 = f32[32,16,128]{2,1,0:T(8,128)} custom-call(f32[16,4096]{1,0:T(8,128)} %temp.1, s32[1,4096]{1,0:T(1,128)} %index.1), custom_call_target="tpu_custom_call" | custom-call | tf_op jit(solution)/shard_map/pallas_call | solution.py:210
  6.7 22.9 %all_to_all.5 = f32[128,4,128]{2,1,0:T(4,128)} all-to-all(f32[128,4,128]{2,1,0:T(4,128)} %bitcast.7), channel_id=1, replica_groups=mesh['row'=8,'col'=16] {'row','col'}, dimensions={0} | all-to-all | bytes 524288 | tf_op jit(solution)/shard_map/all_to_all | solution.py:213
  29.6 21.4 %shard_map.101 = (f32[48,4096]{1,0:T(8,128)}, f32[48,256]{1,0:T(8,128)}) custom-call(f32[32,16,128]{2,1,0:T(8,128)} %bitcast.6, s32[4,4352]{1,0:T(4,128)} %slot.1, f32[4,4352]{1,0:T(4,128)} %weight.1, bf16[48,4352]{1,0:T(8,128)(2,1)} %bitcast.8, f32[3,4352]{1,0:T(4,128)} %expansion.1, bf16[96,96,128]{2,1,0:T(8,128)(2,1)} %tangent.1, s32[32,128]{1,0:T(8,128)} %connect.3), custom_call_target="tpu_custom_call" | custom-call | tf_op jit(solution)/shard_map/pallas_call | solution.py:215
  51.0 0.8 %fusion = (f32[48,128]{1,0:T(8,128)S(1)}, f32[48,128]{1,0:T(8,128)S(1)}) fusion(f32[48,256]{1,0:T(8,128)} %get-tuple-element.8), kind=kLoop, calls=%fused_computation | loop fusion | bytes 98304 | tf_op jit(solution)/shard_map/slice | solution.py:227
  51.7 1.3 %collective-permute-start.1 = (f32[48,128]{1,0:T(8,128)S(1)}, f32[48,128]{1,0:T(8,128)S(1)}, u32[]{:S(2)}, u32[]{:S(2)}) collective-permute-start(f32[48,128]{1,0:T(8,128)S(1)} %get-tuple-element.9), channel_id=1, source_target_pairs={{1,0},{2,1},{3,2},{4,3},{5,4},{6,5},{7,6},{8,7},{9,8},{10,9},{11,1... | collective-permute-start | bytes 73736 | tf_op jit(solution)/shard_map/ppermute | solution.py:205
  53.0 4.0 %collective-permute-start = (f32[48,128]{1,0:T(8,128)S(1)}, f32[48,128]{1,0:T(8,128)S(1)}, u32[]{:S(2)}, u32[]{:S(2)}) collective-permute-start(f32[48,128]{1,0:T(8,128)S(1)} %get-tuple-element.10), channel_id=1, source_target_pairs={{0,1},{1,2},{2,3},{3,4},{4,5},{5,6},{6,7},{7,8},{8,9},{9,10},{10,1... | collective-permute-start | bytes 73736 | tf_op jit(solution)/shard_map/ppermute | solution.py:205
  57.0 5.5 %shard_map.102.own = f32[48,4096]{1,0:T(8,128)} custom-call(f32[48,4096]{1,0:T(8,128)} %get-tuple-element.7.prod, s32[32,128]{1,0:T(8,128)} %connect.3), custom_call_target="tpu_custom_call" | custom-call | tf_op jit(solution)/shard_map/pallas_call | solution.py:228
  62.5 0.0 collective-permute-done.1.from_upper
  62.5 0.0 copy-start
  62.5 0.0 collective-permute-done.from_lower
  62.5 0.0 copy-start.1
  62.5 0.6 copy-done
  63.1 0.0 copy-done.1
  63.1 2.5 %shard_map.103 = f32[48,4096]{1,0:T(8,128)} custom-call(f32[48,4096]{1,0:T(8,128)} %shard_map.102.own, f32[48,128]{1,0:T(8,128)} %copy-done.1, f32[48,128]{1,0:T(8,128)} %copy-done, s32[1,128]{1,0:T(1,128)} %bitcast.9, s32[1,128]{1,0:T(1,128)} %bitcast.10), custom_call_target="tpu_custom_call" | custom-call | tf_op jit(solution)/shard_map/pallas_call | solution.py:233
Async XLA Ops:
  51.7 10.8 %collective-permute-start.1 = (f32[48,128]{1,0:T(8,128)S(1)}, f32[48,128]{1,0:T(8,128)S(1)}, u32[]{:S(2)}, u32[]{:S(2)}) collective-permute-start(f32[48,128]{1,0:T(8,128)S(1)} %get-tuple-element.9), channel_id=1, source_target_pairs={{1,0},{2,1},{3,2},{4,3},{5,4},{6,5},{7,6},{8,7},{9,8},{10,9},{11,1... | collective-permute-start | bytes 73736 | tf_op jit(solution)/shard_map/ppermute | solution.py:205
  53.0 9.5 %collective-permute-start = (f32[48,128]{1,0:T(8,128)S(1)}, f32[48,128]{1,0:T(8,128)S(1)}, u32[]{:S(2)}, u32[]{:S(2)}) collective-permute-start(f32[48,128]{1,0:T(8,128)S(1)} %get-tuple-element.10), channel_id=1, source_target_pairs={{0,1},{1,2},{2,3},{3,4},{4,5},{5,6},{6,7},{7,8},{8,9},{9,10},{10,1... | collective-permute-start | bytes 73736 | tf_op jit(solution)/shard_map/ppermute | solution.py:205
  62.5 0.6 copy-start
  62.5 0.6 copy-start.1
where the time goes:
time: 65.9 us; the launch traced here: 65.6 us
  Pallas kernels  36 us (55%)
  blocking collectives  22.9 us (35%)
  starting transfers between devices  5.27 us (8%)
  local copies, waits for them, and re-layouts  1.36 us (2%)
    all_to_all x1, blocking collectives, shards(): lax.all_to_all(packed.reshape(128, 4, LANES), AXES, split_axis=0, concat_...  22.9 us
    pallas_call x1, Pallas kernels, shards(): call(main_kernel, (shape((48, 4096), F32), shape((48, WIDE), F32)), [pltp...  21.4 us
    pallas_call x1, Pallas kernels, shards(): call(send_kernel, shape((32, 16, LANES), F32), [pltpu.VMEM((256, 2 * WIDE...  6.68 us
    pallas_call x1, Pallas kernels, shards(): call(owned_kernel, shape((48, 4096), F32), [pltpu.VMEM((2 * 16 * 48, 4096...  5.48 us
    ppermute x2, starting transfers between devices, neighbour(): return lax.ppermute(block, 'col', route)  5.27 us
    pallas_call x1, Pallas kernels, shards(): call(ghost_kernel, shape((48, 4096), F32))  2.45 us
  transfers between devices with their start and end apart: 2, of which 0 were waited for; matrix products, arithmetic and copies ran while one was open for 0% of the time, Pallas kernels for 8%

commit v1 on v0

v1 whole, which is shorter than its diff:
```python
import jax
import jax.numpy as jnp
from jax import lax
from jax.experimental import pallas as pl
from jax.experimental.pallas import tpu as pltpu
from jax.sharding import PartitionSpec as P

F32 = jnp.float32
BF16 = jnp.bfloat16
I32 = jnp.int32
LANES = 128
WIDE = 256
AXES = ("row", "col")
NT = (((1,), (1,)), ((), ()))
VMEM_BYTES = 32 * 2**20


def call(body, outs, scratch=()):
    return pl.pallas_call(
        body,
        out_shape=outs,
        scratch_shapes=scratch,
        compiler_params=pltpu.CompilerParams(vmem_limit_bytes=VMEM_BYTES),
    )


def split(x):
    high = x.astype(BF16)
    return high, (x - high.astype(F32)).astype(BF16)


def one_hot(low, iota):
    return jnp.where(iota == low.astype(F32).astype(BF16), jnp.ones((), BF16), jnp.zeros((), BF16))


def iota_of(columns):
    return lax.broadcasted_iota(I32, (WIDE, columns), 0).astype(F32).astype(BF16)


def choose(stacked, high, rows):
    out = stacked[0:rows]
    for h in range(1, stacked.shape[0] // rows):
        out = jnp.where(high == h, stacked[rows * h : rows * (h + 1)], out)
    return out


def swap_blocks(x):
    row = lax.broadcasted_iota(I32, x.shape, 0) >> 2
    col = lax.broadcasted_iota(I32, x.shape, 1) >> 5
    out = x
    for d in range(1, 4):
        moved = pltpu.roll(pltpu.roll(x, 16 - 4 * d, 0), 32 * d, 1)
        out = jnp.where(((col - row) & 3) == d, moved, out)
    return out


def fill_table(tab, read, blocks):
    for h in range(blocks):
        high, low = split(read(h))
        rows = high.shape[0]
        tab[h * rows : (h + 1) * rows, 0:WIDE] = high
        tab[h * rows : (h + 1) * rows, WIDE : 2 * WIDE] = low


def send_kernel(temp, index, out, tab):
    fill_table(tab, lambda h: temp[:, h * WIDE : (h + 1) * WIDE], temp.shape[1] // WIDE)
    iota = iota_of(WIDE)
    for j in range(index.shape[1] // WIDE):
        idx = index[0:1, j * WIDE : (j + 1) * WIDE]
        hot = one_hot(idx & (WIDE - 1), iota)
        stacked = jnp.dot(tab[...], jnp.concatenate([hot, hot], 0), preferred_element_type=F32)
        got = choose(stacked, idx >> 8, 16)
        out[2 * j] = swap_blocks(got[:, 0:LANES])
        out[2 * j + 1] = swap_blocks(got[:, LANES:])


def main_kernel(arrived, slot, weight, disp, expansion, blocks, connect, prod, lower, upper, tab, tab3, matrices, sem):
    fetch = pltpu.make_async_copy(blocks, matrices, sem)
    fetch.start()
    extent = slot.shape[1]

    def table(h):
        return jnp.concatenate([swap_blocks(arrived[2 * h]), swap_blocks(arrived[2 * h + 1])], 1)

    fill_table(tab, table, arrived.shape[0] // 2)
    iota = iota_of(WIDE)

    for j in range(extent // WIDE):
        js = slice(j * WIDE, (j + 1) * WIDE)
        temp = jnp.zeros((16, WIDE), F32)
        for c in range(4):
            idx = slot[c : c + 1, js]
            hot = one_hot(idx & (WIDE - 1), iota)
            stacked = jnp.dot(tab[...], jnp.concatenate([hot, hot], 0), preferred_element_type=F32)
            temp = temp + weight[c : c + 1, js] * choose(stacked, idx >> 8, 16)
        strain = temp / jnp.sqrt(1.0 + temp * temp)
        for a in range(3):
            d = disp[16 * a : 16 * a + 16, js].astype(F32)
            s = (d - expansion[a : a + 1, js] * strain).astype(BF16)
            tab3[j * 48 + a * 16 : j * 48 + a * 16 + 16, :] = s

    fetch.wait()
    lane = lax.broadcasted_iota(I32, (16, LANES), 1) >> 5
    total = jnp.zeros((48, WIDE), F32)
    for p in range(connect.shape[1] // WIDE):
        idx = connect[0:1, p * WIDE : (p + 1) * WIDE]
        hot = one_hot(idx & (WIDE - 1), iota)
        got = choose(jnp.dot(tab3[...], hot, preferred_element_type=F32), idx >> 8, 48)
        pieces = []
        for half in range(2):
            x = [got[16 * a : 16 * a + 16, half * LANES : (half + 1) * LANES] for a in range(3)]
            y = []
            for u in range(4):
                v = [turn(x[a], a - u) for a in range(3)]
                v = jnp.where(lane == 0, v[0], jnp.where(lane == 1, v[1], v[2])).astype(BF16)
                one = jnp.dot(v[:, 0:96], matrices[p * 8 + half * 4 + u], preferred_element_type=F32)
                y.append(jnp.concatenate([one, jnp.zeros((16, 32), F32)], 1))
            rows = []
            for a in range(3):
                w = [turn(y[u], u - a) for u in range(4)]
                rows.append(jnp.where(lane == 0, w[0], jnp.where(lane == 1, w[1], jnp.where(lane == 2, w[2], w[3]))))
            pieces.append(jnp.concatenate(rows, 0))
        value = jnp.concatenate(pieces, 1)
        prod[:, p * WIDE : (p + 1) * WIDE] = value
        high, low = split(jnp.where((idx >> 8) == extent // WIDE - 1, value, 0.0))
        total = total + lax.dot_general(
            jnp.concatenate([high, low], 1), jnp.concatenate([hot, hot], 1), NT, preferred_element_type=F32
        )
    lower[...] = total[:, 0:LANES]
    upper[...] = total[:, LANES:]


def turn(x, blocks):
    return pltpu.roll(x, (32 * blocks) % LANES, 1) if blocks else x


def final_kernel(prod, connect, from_lower, from_upper, at_lower, at_upper, out):
    blocks = out.shape[1] // WIDE
    iota = iota_of(WIDE)
    zero = jnp.zeros((), BF16)

    def spread(x, idx):
        hot = one_hot(idx & (WIDE - 1), iota)
        high = jnp.broadcast_to((idx >> 8).astype(F32).astype(BF16), x.shape)
        sides = [
            jnp.concatenate([jnp.where(high == jnp.array(h, BF16), part, zero) for h in range(blocks)], 0)
            for part in split(x)
        ]
        return lax.dot_general(
            jnp.concatenate(sides, 1), jnp.concatenate([hot, hot], 1), NT, preferred_element_type=F32
        )

    total = None
    for p in range(connect.shape[1] // WIDE):
        ks = slice(p * WIDE, (p + 1) * WIDE)
        term = spread(prod[:, ks], connect[0:1, ks])
        total = term if total is None else total + term
    ghosts = jnp.concatenate([from_lower[...], from_upper[...]], 1)
    total = total + spread(ghosts, jnp.concatenate([at_lower[...], at_upper[...]], 1))
    for h in range(blocks):
        out[:, h * WIDE : (h + 1) * WIDE] = total[48 * h : 48 * h + 48]


def neighbour(block, distance):
    devices = range(lax.axis_size("col"))
    route = [(i - distance, i) for i in devices if i - distance in devices]
    return lax.ppermute(block, "col", route)


def main_call(*args):
    shape = jax.ShapeDtypeStruct
    whole = pl.BlockSpec(memory_space=pltpu.VMEM)
    return pl.pallas_call(
        main_kernel,
        out_shape=(shape((48, 4096), F32), shape((48, LANES), F32), shape((48, LANES), F32)),
        in_specs=[whole] * 5 + [pl.BlockSpec(memory_space=pl.ANY), whole],
        out_specs=(whole, whole, whole),
        scratch_shapes=[
            pltpu.VMEM((256, 2 * WIDE), BF16),
            pltpu.VMEM((17 * 48, WIDE), BF16),
            pltpu.VMEM((128, 96, 96), BF16),
            pltpu.SemaphoreType.DMA(()),
        ],
        compiler_params=pltpu.CompilerParams(vmem_limit_bytes=VMEM_BYTES),
    )(*args)


def shards(temp_thermal, send_index, interp_slot, interp_weight, disp, expansion, tangent, connect, recv_lower, recv_upper):
    shape = jax.ShapeDtypeStruct
    packed = call(
        send_kernel, shape((32, 16, LANES), F32), [pltpu.VMEM((256, 2 * WIDE), BF16)]
    )(temp_thermal, send_index)
    arrived = lax.all_to_all(packed.reshape(128, 4, LANES), AXES, split_axis=0, concat_axis=0, tiled=True)
    arrived = arrived.reshape(32, 16, LANES)
    links = connect.T.reshape(1, 4096)
    blocks = jnp.transpose(tangent, (2, 1, 0))
    prod, lower, upper = main_call(arrived, interp_slot, interp_weight, disp.reshape(48, -1), expansion, blocks, links)
    from_lower = neighbour(upper, 1)
    from_upper = neighbour(lower, -1)
    result = call(final_kernel, shape((48, 4096), F32))(
        prod, links, from_lower, from_upper, recv_lower.reshape(1, LANES), recv_upper.reshape(1, LANES)
    )
    return result.reshape(3, 16, 4096)


def solution(mesh):
    in_specs = (
        P(None, AXES),
        P(AXES, None),
        P(None, AXES),
        P(None, AXES),
        P(None, None, AXES),
        P(None, AXES),
        P(None, None, AXES),
        P(None, AXES),
        P(AXES),
        P(AXES),
    )
    out_specs = P(None, None, AXES)
    return jax.shard_map(shards, mesh=mesh, in_specs=in_specs, out_specs=out_specs, check_vma=False)
```

time: 65.9 us -> 54.6 us (0.83)
  the two profiles are of different devices: /device:TPU:1 before, /device:TPU:2 now
where the time goes in v1:
time: 54.6 us; the launch traced here: 53.6 us
  Pallas kernels  18.6 us (34%)
  starting transfers between devices  18.5 us (34%)
  local copies, waits for them, and re-layouts  9.54 us (17%)
  waiting for transfers between devices  6.86 us (13%)
    pallas_call x1, Pallas kernels, main_call(): pl.pallas_call(main_kernel, out_shape=(shape((48, 4096), F32), shape((48,...  12 us
    all_to_all x1, starting transfers between devices, shards(): lax.all_to_all(packed.reshape(128, 4, LANES), AXES, split_axis=0, concat_...  10.5 us
    unnamed x17, local copies, waits for them, and re-layouts  8.63 us
    ppermute x2, starting transfers between devices, neighbour(): return lax.ppermute(block, 'col', route)  7.95 us
    all_to_all x1, waiting for transfers between devices, shards(): lax.all_to_all(packed.reshape(128, 4, LANES), AXES, split_axis=0, concat_...  5.37 us
    pallas_call x1, Pallas kernels, shards(): call(final_kernel, shape((48, 4096), F32))  4.52 us
    pallas_call x1, Pallas kernels, shards(): call(send_kernel, shape((32, 16, LANES), F32), [pltpu.VMEM((256, 2 * WIDE...  2.09 us
    ppermute x2, waiting for transfers between devices, neighbour(): return lax.ppermute(block, 'col', route)  1.49 us
  transfers between devices with their start and end apart: 3, of which 2 were waited for; matrix products, arithmetic and copies ran while one was open for 10% of the time, Pallas kernels for 0%

profile of v1, /device:TPU:2, one launch (start us, length us, event | category | flops | bytes accessed | tf_op | source)
XLA Modules:
  0.0 53.6 jit_solution(9163749924902172854)
XLA Ops:
  0.0 0.0 copy-start.1
  0.0 0.9 %copy-done.1 = f32[16,4096]{1,0:T(8,128)S(1)} copy-done((f32[16,4096]{1,0:T(8,128)S(1)}, f32[16,4096]{1,0:T(8,128)}, u32[]{:S(2)}) %copy-start.1) | copy-done | bytes 262168
  1.0 0.0 copy-start.5
  1.0 0.7 %copy-done.5 = s32[1,4096]{1,0:T(1,128)S(1)} copy-done((s32[1,4096]{1,0:T(1,128)S(1)}, s32[1,4096]{1,0:T(1,128)}, u32[]{:S(2)}) %copy-start.5) | copy-done | bytes 16408
  1.7 2.1 %shard_map.100 = f32[32,16,128]{2,1,0:T(8,128)} custom-call(f32[16,4096]{1,0:T(8,128)S(1)} %copy-done.1, s32[1,4096]{1,0:T(1,128)S(1)} %copy-done.5), custom_call_target="tpu_custom_call" | custom-call | tf_op jit(solution)/shard_map/pallas_call | solution.py:190
  3.8 0.0 copy-start.2
  3.8 10.5 %all-to-all-start = ((f32[128,4,128]{2,1,0:T(4,128)}), f32[128,4,128]{2,1,0:T(4,128)S(1)}, u32[]{:S(2)}, u32[]{:S(2)}) async-start(f32[128,4,128]{2,1,0:T(4,128)} %bitcast), calls=%async_computation | async-start | bytes 524288 | tf_op jit(solution)/shard_map/all_to_all | solution.py:193
  14.3 0.8 %copy.14 = s32[128,32]{1,0:T(8,128)S(1)} copy(s32[128,32]{0,1:T(8,128)} %bitcast.13) | data formatting | bytes 32768 | tf_op jit(solution)/shard_map/transpose | solution.py:195
  15.1 0.1 reshape.24.connect
  15.2 4.2 %copy.13 = bf16[96,96,128]{0,1,2:T(8,128)(2,1)S(1)} copy(bf16[96,96,128]{2,1,0:T(8,128)(2,1)} %param.16) | data formatting | bytes 4718592 | tf_op args[6]
  19.4 0.0 copy-start.6
  19.4 0.0 copy-start.7
  19.4 5.4 %all-to-all-done = f32[128,4,128]{2,1,0:T(4,128)S(1)} async-done(((f32[128,4,128]{2,1,0:T(4,128)}), f32[128,4,128]{2,1,0:T(4,128)S(1)}, u32[]{:S(2)}, u32[]{:S(2)}) %all-to-all-start) | async-done | bytes 262176 | tf_op jit(solution)/shard_map/all_to_all | solution.py:193
  24.8 0.0 copy-done.2
  24.8 0.0 copy-start
  24.8 1.0 %copy-done = bf16[3,16,4352]{2,1,0:T(8,128)(2,1)S(1)} copy-done((bf16[3,16,4352]{2,1,0:T(8,128)(2,1)S(1)}, bf16[3,16,4352]{2,1,0:T(8,128)(2,1)}, u32[]{:S(2)}) %copy-start) | copy-done | bytes 417816
  25.8 0.0 copy-start.3
  25.8 0.9 %copy-done.3 = f32[4,4352]{1,0:T(4,128)S(1)} copy-done((f32[4,4352]{1,0:T(4,128)S(1)}, f32[4,4352]{1,0:T(4,128)}, u32[]{:S(2)}) %copy-start.3) | copy-done | bytes 69656
  26.7 0.0 copy-start.4
  26.7 0.9 %copy-done.4 = f32[3,4352]{1,0:T(4,128)S(1)} copy-done((f32[3,4352]{1,0:T(4,128)S(1)}, f32[3,4352]{1,0:T(4,128)}, u32[]{:S(2)}) %copy-start.4) | copy-done | bytes 52248
  27.6 12.0 %shard_map.101 = (f32[48,4096]{1,0:T(8,128)S(1)}, f32[48,128]{1,0:T(8,128)S(1)}, f32[48,128]{1,0:T(8,128)S(1)}) custom-call(f32[32,16,128]{2,1,0:T(8,128)S(1)} %bitcast.9, s32[4,4352]{1,0:T(4,128)S(1)} %copy-done.2, f32[4,4352]{1,0:T(4,128)S(1)} %copy-done.3, bf16[48,4352]{1,0:T(8,128)(2,1)S(1)} %bitcast.10, f32[3,4352]{1,0:T(4,128)S(1)} %copy-done.4, ...), custom_call_target="tpu_custom_call" | custom-call | tf_op jit(solution)/shard_map/pallas_call | solution.py:173
  39.6 2.8 %collective-permute-start = (f32[48,128]{1,0:T(8,128)S(1)}, f32[48,128]{1,0:T(8,128)S(1)}, u32[]{:S(2)}, u32[]{:S(2)}) collective-permute-start(f32[48,128]{1,0:T(8,128)S(1)} %get-tuple-element.9), channel_id=1, source_target_pairs={{0,1},{1,2},{2,3},{3,4},{4,5},{5,6},{6,7},{7,8},{8,9},{9,10},{10,1... | collective-permute-start | bytes 73736 | tf_op jit(solution)/shard_map/ppermute | solution.py:167
  42.4 5.2 %collective-permute-start.1 = (f32[48,128]{1,0:T(8,128)S(1)}, f32[48,128]{1,0:T(8,128)S(1)}, u32[]{:S(2)}, u32[]{:S(2)}) collective-permute-start(f32[48,128]{1,0:T(8,128)S(1)} %get-tuple-element.10), channel_id=1, source_target_pairs={{1,0},{2,1},{3,2},{4,3},{5,4},{6,5},{7,6},{8,7},{9,8},{10,9},{11,1... | collective-permute-start | bytes 73736 | tf_op jit(solution)/shard_map/ppermute | solution.py:167
  47.6 0.0 collective-permute-done.from_lower
  47.6 1.5 %collective-permute-done.1.from_upper = f32[48,128]{1,0:T(8,128)S(1)} collective-permute-done((f32[48,128]{1,0:T(8,128)S(1)}, f32[48,128]{1,0:T(8,128)S(1)}, u32[]{:S(2)}, u32[]{:S(2)}) %collective-permute-start.1) | collective-permute-done | bytes 24608 | tf_op jit(solution)/shard_map/ppermute | solution.py:167
  49.1 0.0 copy-done.6
  49.1 0.0 copy-done.7
  49.1 4.5 %shard_map.102 = f32[48,4096]{1,0:T(8,128)} custom-call(f32[48,4096]{1,0:T(8,128)S(1)} %get-tuple-element.8.prod, s32[1,4096]{1,0:T(1,128)S(1)} %reshape.24.connect, f32[48,128]{1,0:T(8,128)S(1)} %collective-permute-done.from_lower, f32[48,128]{1,0:T(8,128)S(1)} %collective-permute-done.1.from_upper, s32[1,128]{1,0:T(1,128)S(1)} %bitcast.11, ...), custom_call_target="tpu_custom_call" | custom-call | tf_op jit(solution)/shard_map/pallas_call | solution.py:200
Async XLA Ops:
  0.0 0.9 %copy-start.1 = (f32[16,4096]{1,0:T(8,128)S(1)}, f32[16,4096]{1,0:T(8,128)}, u32[]{:S(2)}) copy-start(f32[16,4096]{1,0:T(8,128)} %temp.1) | copy-start | bytes 786436
  1.0 0.7 %copy-start.5 = (s32[1,4096]{1,0:T(1,128)S(1)}, s32[1,4096]{1,0:T(1,128)}, u32[]{:S(2)}) copy-start(s32[1,4096]{1,0:T(1,128)} %index.1) | copy-start | bytes 49156
  3.8 21.1 %copy-start.2 = (s32[4,4352]{1,0:T(4,128)S(1)}, s32[4,4352]{1,0:T(4,128)}, u32[]{:S(2)}) copy-start(s32[4,4352]{1,0:T(4,128)} %slot.1) | copy-start | bytes 208900
  3.8 21.0 %all-to-all-start = ((f32[128,4,128]{2,1,0:T(4,128)}), f32[128,4,128]{2,1,0:T(4,128)S(1)}, u32[]{:S(2)}, u32[]{:S(2)}) async-start(f32[128,4,128]{2,1,0:T(4,128)} %bitcast), calls=%async_computation | async-start | bytes 524288 | tf_op jit(solution)/shard_map/all_to_all | solution.py:193
  19.4 29.7 %copy-start.6 = (s32[128]{0:T(128)S(1)}, s32[128]{0:T(128)}, u32[]{:S(2)}) copy-start(s32[128]{0:T(128)} %param.18) | copy-start | bytes 1540
  19.4 29.7 %copy-start.7 = (s32[128]{0:T(128)S(1)}, s32[128]{0:T(128)}, u32[]{:S(2)}) copy-start(s32[128]{0:T(128)} %param.19) | copy-start | bytes 1540
  24.8 1.0 %copy-start = (bf16[3,16,4352]{2,1,0:T(8,128)(2,1)S(1)}, bf16[3,16,4352]{2,1,0:T(8,128)(2,1)}, u32[]{:S(2)}) copy-start(bf16[3,16,4352]{2,1,0:T(8,128)(2,1)} %param.14) | copy-start | bytes 1253380
  25.8 0.9 %copy-start.3 = (f32[4,4352]{1,0:T(4,128)S(1)}, f32[4,4352]{1,0:T(4,128)}, u32[]{:S(2)}) copy-start(f32[4,4352]{1,0:T(4,128)} %weight.1) | copy-start | bytes 208900
  26.7 0.9 %copy-start.4 = (f32[3,4352]{1,0:T(4,128)S(1)}, f32[3,4352]{1,0:T(4,128)}, u32[]{:S(2)}) copy-start(f32[3,4352]{1,0:T(4,128)} %expansion.1) | copy-start | bytes 156676
  39.6 8.0 %collective-permute-start = (f32[48,128]{1,0:T(8,128)S(1)}, f32[48,128]{1,0:T(8,128)S(1)}, u32[]{:S(2)}, u32[]{:S(2)}) collective-permute-start(f32[48,128]{1,0:T(8,128)S(1)} %get-tuple-element.9), channel_id=1, source_target_pairs={{0,1},{1,2},{2,3},{3,4},{4,5},{5,6},{6,7},{7,8},{8,9},{9,10},{10,1... | collective-permute-start | bytes 73736 | tf_op jit(solution)/shard_map/ppermute | solution.py:167
  42.4 6.7 %collective-permute-start.1 = (f32[48,128]{1,0:T(8,128)S(1)}, f32[48,128]{1,0:T(8,128)S(1)}, u32[]{:S(2)}, u32[]{:S(2)}) collective-permute-start(f32[48,128]{1,0:T(8,128)S(1)} %get-tuple-element.10), channel_id=1, source_target_pairs={{1,0},{2,1},{3,2},{4,3},{5,4},{6,5},{7,6},{8,7},{9,8},{10,9},{11,1... | collective-permute-start | bytes 73736 | tf_op jit(solution)/shard_map/ppermute | solution.py:167

commit v2 on v1

--- a/solution.py
+++ b/solution.py
@@ -15,15 +15,6 @@
 VMEM_BYTES = 32 * 2**20
 
 
-def call(body, outs, scratch=()):
-    return pl.pallas_call(
-        body,
-        out_shape=outs,
-        scratch_shapes=scratch,
-        compiler_params=pltpu.CompilerParams(vmem_limit_bytes=VMEM_BYTES),
-    )
-
-
 def split(x):
     high = x.astype(BF16)
     return high, (x - high.astype(F32)).astype(BF16)
@@ -54,17 +45,29 @@
     return out
 
 
-def fill_table(tab, read, blocks):
-    for h in range(blocks):
-        high, low = split(read(h))
-        rows = high.shape[0]
-        tab[h * rows : (h + 1) * rows, 0:WIDE] = high
-        tab[h * rows : (h + 1) * rows, WIDE : 2 * WIDE] = low
-
-
-def send_kernel(temp, index, out, tab):
-    fill_table(tab, lambda h: temp[:, h * WIDE : (h + 1) * WIDE], temp.shape[1] // WIDE)
+def fill_block(tab, h, block):
+    rows = block.shape[0]
+    high, low = split(block)
+    tab[h * rows : (h + 1) * rows, 0:WIDE] = high
+    tab[h * rows : (h + 1) * rows, WIDE : 2 * WIDE] = low
+
+
+def send_kernel(temp_hbm, index_hbm, out, tab, temp, index, sems):
+    parts = 4
+    width = temp.shape[1] // parts
+    copies = [
+        pltpu.make_async_copy(temp_hbm.at[:, pl.ds(i * width, width)], temp.at[:, pl.ds(i * width, width)], sems.at[i])
+        for i in range(parts)
+    ]
+    copies.append(pltpu.make_async_copy(index_hbm, index, sems.at[parts]))
+    for copy in copies:
+        copy.start()
     iota = iota_of(WIDE)
+    for h in range(temp.shape[1] // WIDE):
+        if h * WIDE % width == 0:
+            copies[h * WIDE // width].wait()
+        fill_block(tab, h, temp[:, h * WIDE : (h + 1) * WIDE])
+    copies[parts].wait()
     for j in range(index.shape[1] // WIDE):
         idx = index[0:1, j * WIDE : (j + 1) * WIDE]
         hot = one_hot(idx & (WIDE - 1), iota)
@@ -74,16 +77,22 @@
         out[2 * j + 1] = swap_blocks(got[:, LANES:])
 
 
-def main_kernel(arrived, slot, weight, disp, expansion, blocks, connect, prod, lower, upper, tab, tab3, matrices, sem):
-    fetch = pltpu.make_async_copy(blocks, matrices, sem)
-    fetch.start()
+def main_kernel(
+    arrived, slot_hbm, weight_hbm, disp_hbm, expansion_hbm, blocks, connect,
+    prod, lower, upper,
+    tab, tab3, slot, weight, disp, expansion, matrices, sems,
+):
+    pairs = ((slot_hbm, slot), (weight_hbm, weight), (expansion_hbm, expansion), (disp_hbm, disp), (blocks, matrices))
+    copies = [pltpu.make_async_copy(source, place, sems.at[i]) for i, (source, place) in enumerate(pairs)]
+    for copy in copies:
+        copy.start()
     extent = slot.shape[1]
 
-    def table(h):
-        return jnp.concatenate([swap_blocks(arrived[2 * h]), swap_blocks(arrived[2 * h + 1])], 1)
-
-    fill_table(tab, table, arrived.shape[0] // 2)
+    for h in range(arrived.shape[0] // 2):
+        fill_block(tab, h, jnp.concatenate([swap_blocks(arrived[2 * h]), swap_blocks(arrived[2 * h + 1])], 1))
     iota = iota_of(WIDE)
+    for copy in copies[0:4]:
+        copy.wait()
 
     for j in range(extent // WIDE):
         js = slice(j * WIDE, (j + 1) * WIDE)
@@ -99,7 +108,7 @@
             s = (d - expansion[a : a + 1, js] * strain).astype(BF16)
             tab3[j * 48 + a * 16 : j * 48 + a * 16 + 16, :] = s
 
-    fetch.wait()
+    copies[4].wait()
     lane = lax.broadcasted_iota(I32, (16, LANES), 1) >> 5
     total = jnp.zeros((48, WIDE), F32)
     for p in range(connect.shape[1] // WIDE):
@@ -134,71 +143,95 @@
     return pltpu.roll(x, (32 * blocks) % LANES, 1) if blocks else x
 
 
-def final_kernel(prod, connect, from_lower, from_upper, at_lower, at_upper, out):
+def spread(x, idx, blocks):
+    zero = jnp.zeros((), BF16)
+    hot = one_hot(idx & (WIDE - 1), iota_of(WIDE))
+    high = jnp.broadcast_to((idx >> 8).astype(F32).astype(BF16), x.shape)
+    sides = [
+        jnp.concatenate([jnp.where(high == jnp.array(h, BF16), part, zero) for h in range(blocks)], 0)
+        for part in split(x)
+    ]
+    return lax.dot_general(
+        jnp.concatenate(sides, 1), jnp.concatenate([hot, hot], 1), NT, preferred_element_type=F32
+    )
+
+
+def owned_kernel(prod, connect, out):
     blocks = out.shape[1] // WIDE
-    iota = iota_of(WIDE)
-    zero = jnp.zeros((), BF16)
-
-    def spread(x, idx):
-        hot = one_hot(idx & (WIDE - 1), iota)
-        high = jnp.broadcast_to((idx >> 8).astype(F32).astype(BF16), x.shape)
-        sides = [
-            jnp.concatenate([jnp.where(high == jnp.array(h, BF16), part, zero) for h in range(blocks)], 0)
-            for part in split(x)
-        ]
-        return lax.dot_general(
-            jnp.concatenate(sides, 1), jnp.concatenate([hot, hot], 1), NT, preferred_element_type=F32
-        )
-
     total = None
     for p in range(connect.shape[1] // WIDE):
         ks = slice(p * WIDE, (p + 1) * WIDE)
-        term = spread(prod[:, ks], connect[0:1, ks])
+        term = spread(prod[:, ks], connect[0:1, ks], blocks)
         total = term if total is None else total + term
-    ghosts = jnp.concatenate([from_lower[...], from_upper[...]], 1)
-    total = total + spread(ghosts, jnp.concatenate([at_lower[...], at_upper[...]], 1))
     for h in range(blocks):
         out[:, h * WIDE : (h + 1) * WIDE] = total[48 * h : 48 * h + 48]
 
 
+def ghost_kernel(own, from_lower, from_upper, at, out):
+    blocks = out.shape[1] // WIDE
+    total = spread(jnp.concatenate([from_lower[...], from_upper[...]], 1), at[...], blocks)
+    for h in range(blocks):
+        hs = slice(h * WIDE, (h + 1) * WIDE)
+        out[:, hs] = own[:, hs] + total[48 * h : 48 * h + 48]
+
+
 def neighbour(block, distance):
-    devices = range(lax.axis_size("col"))
-    route = [(i - distance, i) for i in devices if i - distance in devices]
-    return lax.ppermute(block, "col", route)
-
-
-def main_call(*args):
+    count = lax.axis_size("col")
+    return lax.ppermute(block, "col", [(i, (i + distance) % count) for i in range(count)])
+
+
+def shards(temp_thermal, send_index, interp_slot, interp_weight, disp, expansion, tangent, connect, recv_lower, recv_upper):
     shape = jax.ShapeDtypeStruct
-    whole = pl.BlockSpec(memory_space=pltpu.VMEM)
-    return pl.pallas_call(
-        main_kernel,
-        out_shape=(shape((48, 4096), F32), shape((48, LANES), F32), shape((48, LANES), F32)),
-        in_specs=[whole] * 5 + [pl.BlockSpec(memory_space=pl.ANY), whole],
-        out_specs=(whole, whole, whole),
+    here = pl.BlockSpec(memory_space=pltpu.VMEM)
+    away = pl.BlockSpec(memory_space=pltpu.HBM)
+    free = pl.BlockSpec(memory_space=pl.ANY)
+    keep = lambda x: pltpu.with_memory_space_constraint(x, pltpu.HBM)
+    params = pltpu.CompilerParams(vmem_limit_bytes=VMEM_BYTES)
+    packed = pl.pallas_call(
+        send_kernel,
+        out_shape=shape((32, 16, LANES), F32),
+        in_specs=[away, away],
+        out_specs=here,
         scratch_shapes=[
             pltpu.VMEM((256, 2 * WIDE), BF16),
-            pltpu.VMEM((17 * 48, WIDE), BF16),
-            pltpu.VMEM((128, 96, 96), BF16),
-            pltpu.SemaphoreType.DMA(()),
+            pltpu.VMEM((16, 4096), F32),
+            pltpu.VMEM((1, 4096), I32),
+            pltpu.SemaphoreType.DMA((5,)),
         ],
-        compiler_params=pltpu.CompilerParams(vmem_limit_bytes=VMEM_BYTES),
-    )(*args)
-
-
-def shards(temp_thermal, send_index, interp_slot, interp_weight, disp, expansion, tangent, connect, recv_lower, recv_upper):
-    shape = jax.ShapeDtypeStruct
-    packed = call(
-        send_kernel, shape((32, 16, LANES), F32), [pltpu.VMEM((256, 2 * WIDE), BF16)]
-    )(temp_thermal, send_index)
+        compiler_params=params,
+    )(keep(temp_thermal), keep(send_index))
     arrived = lax.all_to_all(packed.reshape(128, 4, LANES), AXES, split_axis=0, concat_axis=0, tiled=True)
     arrived = arrived.reshape(32, 16, LANES)
     links = connect.T.reshape(1, 4096)
     blocks = jnp.transpose(tangent, (2, 1, 0))
-    prod, lower, upper = main_call(arrived, interp_slot, interp_weight, disp.reshape(48, -1), expansion, blocks, links)
+    col = lax.axis_index("col")
+    at = jnp.concatenate(
+        [jnp.where(col > 0, recv_lower, -1), jnp.where(col < lax.axis_size("col") - 1, recv_upper, -1)]
+    ).reshape(1, WIDE)
+    prod, lower, upper = pl.pallas_call(
+        main_kernel,
+        out_shape=(shape((48, 4096), F32), shape((48, LANES), F32), shape((48, LANES), F32)),
+        in_specs=[here, away, away, away, away, free, here],
+        out_specs=(here, here, here),
+        scratch_shapes=[
+            pltpu.VMEM((256, 2 * WIDE), BF16),
+            pltpu.VMEM((17 * 48, WIDE), BF16),
+            pltpu.VMEM((4, 4352), I32),
+            pltpu.VMEM((4, 4352), F32),
+            pltpu.VMEM((48, 4352), BF16),
+            pltpu.VMEM((3, 4352), F32),
+            pltpu.VMEM((128, 96, 96), BF16),
+            pltpu.SemaphoreType.DMA((5,)),
+        ],
+        compiler_params=params,
+    )(
+        arrived, keep(interp_slot), keep(interp_weight), keep(disp.reshape(48, -1)), keep(expansion), blocks, links
+    )
     from_lower = neighbour(upper, 1)
     from_upper = neighbour(lower, -1)
-    result = call(final_kernel, shape((48, 4096), F32))(
-        prod, links, from_lower, from_upper, recv_lower.reshape(1, LANES), recv_upper.reshape(1, LANES)
+    own = pl.pallas_call(owned_kernel, out_shape=shape((48, 4096), F32), compiler_params=params)(prod, links)
+    result = pl.pallas_call(ghost_kernel, out_shape=shape((48, 4096), F32), compiler_params=params)(
+        own, from_lower, from_upper, at
     )
     return result.reshape(3, 16, 4096)
 

time: 54.6 us -> 48.4 us (0.89)
  the two profiles are of different devices: /device:TPU:2 before, /device:TPU:0 now
where the time goes in v2:
time: 48.4 us; the launch traced here: 48.1 us
  Pallas kernels  20.6 us (43%)
  starting transfers between devices  16.6 us (34%)
  waiting for transfers between devices  6.45 us (13%)
  local copies, waits for them, and re-layouts  4.39 us (9%)
    pallas_call x1, Pallas kernels, shards(): pl.pallas_call(main_kernel, out_shape=(shape((48, 4096), F32), shape((48,...  12.8 us
    all_to_all x1, starting transfers between devices, shards(): lax.all_to_all(packed.reshape(128, 4, LANES), AXES, split_axis=0, concat_...  11.1 us
    all_to_all x1, waiting for transfers between devices, shards(): lax.all_to_all(packed.reshape(128, 4, LANES), AXES, split_axis=0, concat_...  6.44 us
    ppermute x2, starting transfers between devices, neighbour(): lax.ppermute(block, 'col', [(i, (i + distance) % count) for i in range(co...  5.42 us
    unnamed x7, local copies, waits for them, and re-layouts  4.2 us
    pallas_call x1, Pallas kernels, shards(): pl.pallas_call(owned_kernel, out_shape=shape((48, 4096), F32), compiler_p...  3.43 us
    pallas_call x1, Pallas kernels, shards(): pl.pallas_call(send_kernel, out_shape=shape((32, 16, LANES), F32), in_spe...  3.06 us
    pallas_call x1, Pallas kernels, shards(): pl.pallas_call(ghost_kernel, out_shape=shape((48, 4096), F32), compiler_p...  1.29 us
  transfers between devices with their start and end apart: 3, of which 1 were waited for; matrix products, arithmetic and copies ran while one was open for 9% of the time, Pallas kernels for 7%

profile of v2, /device:TPU:0, one launch (start us, length us, event | category | flops | bytes accessed | tf_op | source)
XLA Modules:
  0.0 48.1 jit_solution(8761146947582205969)
XLA Ops:
  0.0 3.1 %shard_map.100 = f32[32,16,128]{2,1,0:T(8,128)} custom-call(f32[16,4096]{1,0:T(8,128)} %temp_hbm.1, s32[1,4096]{1,0:T(1,128)} %index_hbm.1), custom_call_target="tpu_custom_call" | custom-call | tf_op jit(solution)/shard_map/pallas_call | solution.py:190
  3.1 0.0 copy-start
  3.1 0.0 copy-start.1
  3.1 0.0 copy-start.2
  3.1 11.1 %all-to-all-start = ((f32[128,4,128]{2,1,0:T(4,128)}), f32[128,4,128]{2,1,0:T(4,128)S(1)}, u32[]{:S(2)}, u32[]{:S(2)}) async-start(f32[128,4,128]{2,1,0:T(4,128)} %bitcast), calls=%async_computation | async-start | bytes 524288 | tf_op jit(solution)/shard_map/all_to_all | solution.py:203
  14.3 4.2 %copy.13 = bf16[96,96,128]{0,1,2:T(8,128)(2,1)S(1)} copy(bf16[96,96,128]{2,1,0:T(8,128)(2,1)} %param.16) | data formatting | bytes 4718592 | tf_op args[6]
  18.4 0.0 copy-done
  18.5 0.1 copy.14
  18.6 0.1 reshape.21.connect
  18.7 0.0 copy-done.1
  18.7 0.0 copy-done.2
  18.7 6.4 %all-to-all-done = f32[128,4,128]{2,1,0:T(4,128)S(1)} async-done(((f32[128,4,128]{2,1,0:T(4,128)}), f32[128,4,128]{2,1,0:T(4,128)S(1)}, u32[]{:S(2)}, u32[]{:S(2)}) %all-to-all-start) | async-done | bytes 262176 | tf_op jit(solution)/shard_map/all_to_all | solution.py:203
  25.1 12.8 %shard_map.101 = (f32[48,4096]{1,0:T(8,128)S(1)}, f32[48,128]{1,0:T(8,128)S(1)}, f32[48,128]{1,0:T(8,128)S(1)}) custom-call(f32[32,16,128]{2,1,0:T(8,128)S(1)} %bitcast.8, s32[4,4352]{1,0:T(4,128)} %slot_hbm.1, f32[4,4352]{1,0:T(4,128)} %weight_hbm.1, bf16[48,4352]{1,0:T(8,128)(2,1)} %bitcast.10, f32[3,4352]{1,0:T(4,128)} %expansion_hbm.1, ...), custom_call_target="tpu_custom_call" | custom-call | tf_op jit(solution)/shard_map/pallas_call | solution.py:211
  37.9 0.9 %collective-permute-start = (f32[48,128]{1,0:T(8,128)S(1)}, f32[48,128]{1,0:T(8,128)S(1)}, u32[]{:S(2)}, u32[]{:S(2)}) collective-permute-start(f32[48,128]{1,0:T(8,128)S(1)} %get-tuple-element.9), channel_id=1, source_target_pairs={{0,1},{1,2},{2,3},{3,4},{4,5},{5,6},{6,7},{7,8},{8,9},{9,10},{10,1... | collective-permute-start | bytes 73736 | tf_op jit(solution)/shard_map/ppermute | solution.py:180
  38.9 4.5 %collective-permute-start.1 = (f32[48,128]{1,0:T(8,128)S(1)}, f32[48,128]{1,0:T(8,128)S(1)}, u32[]{:S(2)}, u32[]{:S(2)}) collective-permute-start(f32[48,128]{1,0:T(8,128)S(1)} %get-tuple-element.10), channel_id=1, source_target_pairs={{0,15},{1,0},{2,1},{3,2},{4,3},{5,4},{6,5},{7,6},{8,7},{9,8},{10,9... | collective-permute-start | bytes 73736 | tf_op jit(solution)/shard_map/ppermute | solution.py:180
  43.4 3.4 %shard_map.102.own = f32[48,4096]{1,0:T(8,128)S(1)} custom-call(f32[48,4096]{1,0:T(8,128)S(1)} %get-tuple-element.8.prod, s32[1,4096]{1,0:T(1,128)S(1)} %reshape.21.connect), custom_call_target="tpu_custom_call" | custom-call | tf_op jit(solution)/shard_map/pallas_call | solution.py:232
  46.8 0.0 collective-permute-done.from_lower
  46.8 0.0 collective-permute-done.1.from_upper
  46.8 1.3 %shard_map.103 = f32[48,4096]{1,0:T(8,128)} custom-call(f32[48,4096]{1,0:T(8,128)S(1)} %shard_map.102.own, f32[48,128]{1,0:T(8,128)S(1)} %collective-permute-done.from_lower, f32[48,128]{1,0:T(8,128)S(1)} %collective-permute-done.1.from_upper, s32[1,256]{1,0:T(1,128)S(1)} %bitcast.9), custom_call_target="tpu_custom_call" | custom-call | tf_op jit(solution)/shard_map/pallas_call | solution.py:233
  (2 shorter events, 0.0 us)
Async XLA Ops:
  3.1 15.4 %copy-start = (s32[32,128]{1,0:T(8,128)S(1)}, s32[32,128]{1,0:T(8,128)}, u32[]{:S(2)}) copy-start(s32[32,128]{1,0:T(8,128)} %param.17) | copy-start | bytes 49156
  3.1 15.6 %copy-start.1 = (s32[128]{0:T(128)S(1)}, s32[128]{0:T(128)}, u32[]{:S(2)}) copy-start(s32[128]{0:T(128)} %param.19) | copy-start | bytes 1540
  3.1 15.6 %copy-start.2 = (s32[128]{0:T(128)S(1)}, s32[128]{0:T(128)}, u32[]{:S(2)}) copy-start(s32[128]{0:T(128)} %param.18) | copy-start | bytes 1540
  3.1 22.0 %all-to-all-start = ((f32[128,4,128]{2,1,0:T(4,128)}), f32[128,4,128]{2,1,0:T(4,128)S(1)}, u32[]{:S(2)}, u32[]{:S(2)}) async-start(f32[128,4,128]{2,1,0:T(4,128)} %bitcast), calls=%async_computation | async-start | bytes 524288 | tf_op jit(solution)/shard_map/all_to_all | solution.py:203
  37.9 8.9 %collective-permute-start = (f32[48,128]{1,0:T(8,128)S(1)}, f32[48,128]{1,0:T(8,128)S(1)}, u32[]{:S(2)}, u32[]{:S(2)}) collective-permute-start(f32[48,128]{1,0:T(8,128)S(1)} %get-tuple-element.9), channel_id=1, source_target_pairs={{0,1},{1,2},{2,3},{3,4},{4,5},{5,6},{6,7},{7,8},{8,9},{9,10},{10,1... | collective-permute-start | bytes 73736 | tf_op jit(solution)/shard_map/ppermute | solution.py:180
  38.9 8.0 %collective-permute-start.1 = (f32[48,128]{1,0:T(8,128)S(1)}, f32[48,128]{1,0:T(8,128)S(1)}, u32[]{:S(2)}, u32[]{:S(2)}) collective-permute-start(f32[48,128]{1,0:T(8,128)S(1)} %get-tuple-element.10), channel_id=1, source_target_pairs={{0,15},{1,0},{2,1},{3,2},{4,3},{5,4},{6,5},{7,6},{8,7},{9,8},{10,9... | collective-permute-start | bytes 73736 | tf_op jit(solution)/shard_map/ppermute | solution.py:180

commit v3 on v2

--- a/solution.py
+++ b/solution.py
@@ -80,7 +80,7 @@
 def main_kernel(
     arrived, slot_hbm, weight_hbm, disp_hbm, expansion_hbm, blocks, connect,
     prod, lower, upper,
-    tab, tab3, slot, weight, disp, expansion, matrices, sems,
+    tab, tab3, slot, weight, disp, expansion, matrices, vec, sems,
 ):
     pairs = ((slot_hbm, slot), (weight_hbm, weight), (expansion_hbm, expansion), (disp_hbm, disp), (blocks, matrices))
     copies = [pltpu.make_async_copy(source, place, sems.at[i]) for i, (source, place) in enumerate(pairs)]
@@ -110,11 +110,17 @@
 
     copies[4].wait()
     lane = lax.broadcasted_iota(I32, (16, LANES), 1) >> 5
-    total = jnp.zeros((48, WIDE), F32)
-    for p in range(connect.shape[1] // WIDE):
-        idx = connect[0:1, p * WIDE : (p + 1) * WIDE]
+    count = connect.shape[1] // WIDE
+
+    def indices(p):
+        return connect[0:1, p * WIDE : (p + 1) * WIDE]
+
+    def gather(p):
+        idx = indices(p)
         hot = one_hot(idx & (WIDE - 1), iota)
-        got = choose(jnp.dot(tab3[...], hot, preferred_element_type=F32), idx >> 8, 48)
+        return choose(jnp.dot(tab3[...], hot, preferred_element_type=F32), idx >> 8, 48)
+
+    def multiply(p, got):
         pieces = []
         for half in range(2):
             x = [got[16 * a : 16 * a + 16, half * LANES : (half + 1) * LANES] for a in range(3)]
@@ -131,10 +137,22 @@
             pieces.append(jnp.concatenate(rows, 0))
         value = jnp.concatenate(pieces, 1)
         prod[:, p * WIDE : (p + 1) * WIDE] = value
+
+    def ghosts(p, total):
+        idx = indices(p)
+        hot = one_hot(idx & (WIDE - 1), iota)
+        value = prod[:, p * WIDE : (p + 1) * WIDE]
         high, low = split(jnp.where((idx >> 8) == extent // WIDE - 1, value, 0.0))
-        total = total + lax.dot_general(
-            jnp.concatenate([high, low], 1), jnp.concatenate([hot, hot], 1), NT, preferred_element_type=F32
-        )
+        return total + lax.dot_general(jnp.concatenate([high, low], 0), hot, NT, preferred_element_type=F32)
+
+    total = jnp.zeros((96, WIDE), F32)
+    for p in range(count):
+        vec[:, p * WIDE : (p + 1) * WIDE] = gather(p)
+    for p in range(count):
+        multiply(p, vec[:, p * WIDE : (p + 1) * WIDE])
+    for p in range(count):
+        total = ghosts(p, total)
+    total = total[0:48] + total[48:96]
     lower[...] = total[:, 0:LANES]
     upper[...] = total[:, LANES:]
 
@@ -221,6 +239,7 @@
             pltpu.VMEM((48, 4352), BF16),
             pltpu.VMEM((3, 4352), F32),
             pltpu.VMEM((128, 96, 96), BF16),
+            pltpu.VMEM((48, 4096), F32),
             pltpu.SemaphoreType.DMA((5,)),
         ],
         compiler_params=params,

time: 48.4 us -> 45.7 us (0.944)
  Pallas kernels: 20.6 us -> 17.8 us
    pallas_call x1, Pallas kernels: 12.8 us -> 10 us  [shards(): pl.pallas_call(main_kernel, out_shape=(shape((48, 4096), F32), shape((48,...]
  transfers between devices with their start and end apart: 3 -> 3, of which waited for: 1 -> 1; matrix products, arithmetic and copies ran while one was open for 9% -> 10% of each run, Pallas kernels for 7% -> 8%
where the time goes in v3:
time: 45.7 us; the launch traced here: 45.4 us
  Pallas kernels  17.8 us (39%)
  starting transfers between devices  16.6 us (36%)
  waiting for transfers between devices  6.45 us (14%)
  local copies, waits for them, and re-layouts  4.39 us (10%)
    all_to_all x1, starting transfers between devices, shards(): lax.all_to_all(packed.reshape(128, 4, LANES), AXES, split_axis=0, concat_...  11.1 us
    pallas_call x1, Pallas kernels, shards(): pl.pallas_call(main_kernel, out_shape=(shape((48, 4096), F32), shape((48,...  10 us
    all_to_all x1, waiting for transfers between devices, shards(): lax.all_to_all(packed.reshape(128, 4, LANES), AXES, split_axis=0, concat_...  6.44 us
    ppermute x2, starting transfers between devices, neighbour(): lax.ppermute(block, 'col', [(i, (i + distance) % count) for i in range(co...  5.42 us
    unnamed x7, local copies, waits for them, and re-layouts  4.2 us
    pallas_call x1, Pallas kernels, shards(): pl.pallas_call(owned_kernel, out_shape=shape((48, 4096), F32), compiler_p...  3.44 us
    pallas_call x1, Pallas kernels, shards(): pl.pallas_call(send_kernel, out_shape=shape((32, 16, LANES), F32), in_spe...  3.06 us
    pallas_call x1, Pallas kernels, shards(): pl.pallas_call(ghost_kernel, out_shape=shape((48, 4096), F32), compiler_p...  1.28 us
  transfers between devices with their start and end apart: 3, of which 1 were waited for; matrix products, arithmetic and copies ran while one was open for 10% of the time, Pallas kernels for 8%

profile of v3, /device:TPU:0, one launch (start us, length us, event | category | flops | bytes accessed | tf_op | source)
XLA Modules:
  0.0 45.4 jit_solution(2338683170906345613)
XLA Ops:
  0.0 3.1 %shard_map.100 = f32[32,16,128]{2,1,0:T(8,128)} custom-call(f32[16,4096]{1,0:T(8,128)} %temp_hbm.1, s32[1,4096]{1,0:T(1,128)} %index_hbm.1), custom_call_target="tpu_custom_call" | custom-call | tf_op jit(solution)/shard_map/pallas_call | solution.py:208
  3.1 0.0 copy-start
  3.1 0.0 copy-start.1
  3.1 0.0 copy-start.2
  3.1 11.1 %all-to-all-start = ((f32[128,4,128]{2,1,0:T(4,128)}), f32[128,4,128]{2,1,0:T(4,128)S(1)}, u32[]{:S(2)}, u32[]{:S(2)}) async-start(f32[128,4,128]{2,1,0:T(4,128)} %bitcast), calls=%async_computation | async-start | bytes 524288 | tf_op jit(solution)/shard_map/all_to_all | solution.py:221
  14.3 4.2 %copy.13 = bf16[96,96,128]{0,1,2:T(8,128)(2,1)S(1)} copy(bf16[96,96,128]{2,1,0:T(8,128)(2,1)} %param.16) | data formatting | bytes 4718592 | tf_op args[6]
  18.4 0.0 copy-done
  18.5 0.1 copy.14
  18.6 0.1 reshape.21.connect
  18.7 0.0 copy-done.1
  18.7 0.0 copy-done.2
  18.7 6.4 %all-to-all-done = f32[128,4,128]{2,1,0:T(4,128)S(1)} async-done(((f32[128,4,128]{2,1,0:T(4,128)}), f32[128,4,128]{2,1,0:T(4,128)S(1)}, u32[]{:S(2)}, u32[]{:S(2)}) %all-to-all-start) | async-done | bytes 262176 | tf_op jit(solution)/shard_map/all_to_all | solution.py:221
  25.1 10.0 %shard_map.101 = (f32[48,4096]{1,0:T(8,128)S(1)}, f32[48,128]{1,0:T(8,128)S(1)}, f32[48,128]{1,0:T(8,128)S(1)}) custom-call(f32[32,16,128]{2,1,0:T(8,128)S(1)} %bitcast.8, s32[4,4352]{1,0:T(4,128)} %slot_hbm.1, f32[4,4352]{1,0:T(4,128)} %weight_hbm.1, bf16[48,4352]{1,0:T(8,128)(2,1)} %bitcast.10, f32[3,4352]{1,0:T(4,128)} %expansion_hbm.1, ...), custom_call_target="tpu_custom_call" | custom-call | tf_op jit(solution)/shard_map/pallas_call | solution.py:229
  35.2 0.9 %collective-permute-start = (f32[48,128]{1,0:T(8,128)S(1)}, f32[48,128]{1,0:T(8,128)S(1)}, u32[]{:S(2)}, u32[]{:S(2)}) collective-permute-start(f32[48,128]{1,0:T(8,128)S(1)} %get-tuple-element.9), channel_id=1, source_target_pairs={{0,1},{1,2},{2,3},{3,4},{4,5},{5,6},{6,7},{7,8},{8,9},{9,10},{10,1... | collective-permute-start | bytes 73736 | tf_op jit(solution)/shard_map/ppermute | solution.py:198
  36.1 4.5 %collective-permute-start.1 = (f32[48,128]{1,0:T(8,128)S(1)}, f32[48,128]{1,0:T(8,128)S(1)}, u32[]{:S(2)}, u32[]{:S(2)}) collective-permute-start(f32[48,128]{1,0:T(8,128)S(1)} %get-tuple-element.10), channel_id=1, source_target_pairs={{0,15},{1,0},{2,1},{3,2},{4,3},{5,4},{6,5},{7,6},{8,7},{9,8},{10,9... | collective-permute-start | bytes 73736 | tf_op jit(solution)/shard_map/ppermute | solution.py:198
  40.6 3.4 %shard_map.102.own = f32[48,4096]{1,0:T(8,128)S(1)} custom-call(f32[48,4096]{1,0:T(8,128)S(1)} %get-tuple-element.8.prod, s32[1,4096]{1,0:T(1,128)S(1)} %reshape.21.connect), custom_call_target="tpu_custom_call" | custom-call | tf_op jit(solution)/shard_map/pallas_call | solution.py:251
  44.1 0.0 collective-permute-done.from_lower
  44.1 0.0 collective-permute-done.1.from_upper
  44.1 1.3 %shard_map.103 = f32[48,4096]{1,0:T(8,128)} custom-call(f32[48,4096]{1,0:T(8,128)S(1)} %shard_map.102.own, f32[48,128]{1,0:T(8,128)S(1)} %collective-permute-done.from_lower, f32[48,128]{1,0:T(8,128)S(1)} %collective-permute-done.1.from_upper, s32[1,256]{1,0:T(1,128)S(1)} %bitcast.9), custom_call_target="tpu_custom_call" | custom-call | tf_op jit(solution)/shard_map/pallas_call | solution.py:252
  (2 shorter events, 0.0 us)
Async XLA Ops:
  3.1 15.4 %copy-start = (s32[32,128]{1,0:T(8,128)S(1)}, s32[32,128]{1,0:T(8,128)}, u32[]{:S(2)}) copy-start(s32[32,128]{1,0:T(8,128)} %param.17) | copy-start | bytes 49156
  3.1 15.6 %copy-start.1 = (s32[128]{0:T(128)S(1)}, s32[128]{0:T(128)}, u32[]{:S(2)}) copy-start(s32[128]{0:T(128)} %param.19) | copy-start | bytes 1540
  3.1 15.6 %copy-start.2 = (s32[128]{0:T(128)S(1)}, s32[128]{0:T(128)}, u32[]{:S(2)}) copy-start(s32[128]{0:T(128)} %param.18) | copy-start | bytes 1540
  3.1 22.0 %all-to-all-start = ((f32[128,4,128]{2,1,0:T(4,128)}), f32[128,4,128]{2,1,0:T(4,128)S(1)}, u32[]{:S(2)}, u32[]{:S(2)}) async-start(f32[128,4,128]{2,1,0:T(4,128)} %bitcast), calls=%async_computation | async-start | bytes 524288 | tf_op jit(solution)/shard_map/all_to_all | solution.py:221
  35.2 8.9 %collective-permute-start = (f32[48,128]{1,0:T(8,128)S(1)}, f32[48,128]{1,0:T(8,128)S(1)}, u32[]{:S(2)}, u32[]{:S(2)}) collective-permute-start(f32[48,128]{1,0:T(8,128)S(1)} %get-tuple-element.9), channel_id=1, source_target_pairs={{0,1},{1,2},{2,3},{3,4},{4,5},{5,6},{6,7},{7,8},{8,9},{9,10},{10,1... | collective-permute-start | bytes 73736 | tf_op jit(solution)/shard_map/ppermute | solution.py:198
  36.1 8.0 %collective-permute-start.1 = (f32[48,128]{1,0:T(8,128)S(1)}, f32[48,128]{1,0:T(8,128)S(1)}, u32[]{:S(2)}, u32[]{:S(2)}) collective-permute-start(f32[48,128]{1,0:T(8,128)S(1)} %get-tuple-element.10), channel_id=1, source_target_pairs={{0,15},{1,0},{2,1},{3,2},{4,3},{5,4},{6,5},{7,6},{8,7},{9,8},{10,9... | collective-permute-start | bytes 73736 | tf_op jit(solution)/shard_map/ppermute | solution.py:198

commit v4 on v3

--- a/solution.py
+++ b/solution.py
@@ -29,10 +29,12 @@
 
 
 def choose(stacked, high, rows):
-    out = stacked[0:rows]
+    high = jnp.broadcast_to(high, (8, high.shape[1]))
+    out = [stacked[r : r + 8] for r in range(0, rows, 8)]
     for h in range(1, stacked.shape[0] // rows):
-        out = jnp.where(high == h, stacked[rows * h : rows * (h + 1)], out)
-    return out
+        here = high == h
+        out = [jnp.where(here, stacked[rows * h + 8 * i : rows * h + 8 * i + 8], x) for i, x in enumerate(out)]
+    return jnp.concatenate(out, 0)
 
 
 def swap_blocks(x):
@@ -45,11 +47,29 @@
     return out
 
 
-def fill_block(tab, h, block):
-    rows = block.shape[0]
-    high, low = split(block)
-    tab[h * rows : (h + 1) * rows, 0:WIDE] = high
-    tab[h * rows : (h + 1) * rows, WIDE : 2 * WIDE] = low
+def code(block):
+    high = block.astype(BF16).astype(F32)
+    rest = (block - high) / jnp.where(high != 0.0, high, 1.0)
+    rest = jnp.clip(jnp.floor(rest * 2048.0 + 8.0), 0.0, 15.0)
+    return high, rest[0:8] * 16.0 + rest[8:16]
+
+
+def fill_pair(tab, h, first, second):
+    base = 2 * tab.shape[0] // 3
+    (high, rest), (high2, rest2) = code(first), code(second)
+    tab[16 * h : 16 * h + 32, :] = jnp.concatenate([high, high2], 0).astype(BF16)
+    tab[base + 8 * h : base + 8 * h + 16, :] = jnp.concatenate([rest, rest2], 0).astype(BF16)
+
+
+def look_up(tab, hot, high):
+    stacked = jnp.dot(tab[...], hot, preferred_element_type=F32)
+    base = 2 * tab.shape[0] // 3
+    value = choose(stacked[0:base], high, 16)
+    both = choose(stacked[base:], high, 8)
+    upper = jnp.floor(both * 0.0625)
+    lower = both - 16.0 * upper
+    unit, shift = 1.0 / 2048.0, 1.0 - 7.5 / 2048.0
+    return jnp.concatenate([value[0:8] * (upper * unit + shift), value[8:16] * (lower * unit + shift)], 0)
 
 
 def send_kernel(temp_hbm, index_hbm, out, tab, temp, index, sems):
@@ -66,13 +86,13 @@
     for h in range(temp.shape[1] // WIDE):
         if h * WIDE % width == 0:
             copies[h * WIDE // width].wait()
-        fill_block(tab, h, temp[:, h * WIDE : (h + 1) * WIDE])
+        if h % 2 == 0:
+            fill_pair(tab, h, temp[:, h * WIDE : (h + 1) * WIDE], temp[:, (h + 1) * WIDE : (h + 2) * WIDE])
     copies[parts].wait()
     for j in range(index.shape[1] // WIDE):
         idx = index[0:1, j * WIDE : (j + 1) * WIDE]
         hot = one_hot(idx & (WIDE - 1), iota)
-        stacked = jnp.dot(tab[...], jnp.concatenate([hot, hot], 0), preferred_element_type=F32)
-        got = choose(stacked, idx >> 8, 16)
+        got = look_up(tab, hot, idx >> 8)
         out[2 * j] = swap_blocks(got[:, 0:LANES])
         out[2 * j + 1] = swap_blocks(got[:, LANES:])
 
@@ -88,8 +108,9 @@
         copy.start()
     extent = slot.shape[1]
 
-    for h in range(arrived.shape[0] // 2):
-        fill_block(tab, h, jnp.concatenate([swap_blocks(arrived[2 * h]), swap_blocks(arrived[2 * h + 1])], 1))
+    for h in range(0, arrived.shape[0] // 2, 2):
+        tiles = [swap_blocks(arrived[2 * h + i]) for i in range(4)]
+        fill_pair(tab, h, jnp.concatenate(tiles[0:2], 1), jnp.concatenate(tiles[2:4], 1))
     iota = iota_of(WIDE)
     for copy in copies[0:4]:
         copy.wait()
@@ -100,8 +121,7 @@
         for c in range(4):
             idx = slot[c : c + 1, js]
             hot = one_hot(idx & (WIDE - 1), iota)
-            stacked = jnp.dot(tab[...], jnp.concatenate([hot, hot], 0), preferred_element_type=F32)
-            temp = temp + weight[c : c + 1, js] * choose(stacked, idx >> 8, 16)
+            temp = temp + weight[c : c + 1, js] * look_up(tab, hot, idx >> 8)
         strain = temp / jnp.sqrt(1.0 + temp * temp)
         for a in range(3):
             d = disp[16 * a : 16 * a + 16, js].astype(F32)
@@ -211,7 +231,7 @@
         in_specs=[away, away],
         out_specs=here,
         scratch_shapes=[
-            pltpu.VMEM((256, 2 * WIDE), BF16),
+            pltpu.VMEM((384, WIDE), BF16),
             pltpu.VMEM((16, 4096), F32),
             pltpu.VMEM((1, 4096), I32),
             pltpu.SemaphoreType.DMA((5,)),
@@ -232,7 +252,7 @@
         in_specs=[here, away, away, away, away, free, here],
         out_specs=(here, here, here),
         scratch_shapes=[
-            pltpu.VMEM((256, 2 * WIDE), BF16),
+            pltpu.VMEM((384, WIDE), BF16),
             pltpu.VMEM((17 * 48, WIDE), BF16),
             pltpu.VMEM((4, 4352), I32),
             pltpu.VMEM((4, 4352), F32),

time: 45.7 us -> 44.3 us (0.969)
  Pallas kernels: 17.8 us -> 16.4 us
    pallas_call x1, Pallas kernels: 10 us -> 8.88 us  [shards(): pl.pallas_call(main_kernel, out_shape=(shape((48, 4096), F32), shape((48,...]
where the time goes in v4:
time: 44.3 us; the launch traced here: 44 us
  starting transfers between devices  16.6 us (37%)
  Pallas kernels  16.4 us (37%)
  waiting for transfers between devices  6.45 us (15%)
  local copies, waits for them, and re-layouts  4.39 us (10%)
    all_to_all x1, starting transfers between devices, shards(): lax.all_to_all(packed.reshape(128, 4, LANES), AXES, split_axis=0, concat_...  11.1 us
    pallas_call x1, Pallas kernels, shards(): pl.pallas_call(main_kernel, out_shape=(shape((48, 4096), F32), shape((48,...  8.88 us
    all_to_all x1, waiting for transfers between devices, shards(): lax.all_to_all(packed.reshape(128, 4, LANES), AXES, split_axis=0, concat_...  6.44 us
    ppermute x2, starting transfers between devices, neighbour(): lax.ppermute(block, 'col', [(i, (i + distance) % count) for i in range(co...  5.42 us
    unnamed x7, local copies, waits for them, and re-layouts  4.2 us
    pallas_call x1, Pallas kernels, shards(): pl.pallas_call(owned_kernel, out_shape=shape((48, 4096), F32), compiler_p...  3.44 us
    pallas_call x1, Pallas kernels, shards(): pl.pallas_call(send_kernel, out_shape=shape((32, 16, LANES), F32), in_spe...  2.83 us
    pallas_call x1, Pallas kernels, shards(): pl.pallas_call(ghost_kernel, out_shape=shape((48, 4096), F32), compiler_p...  1.28 us
  transfers between devices with their start and end apart: 3, of which 1 were waited for; matrix products, arithmetic and copies ran while one was open for 10% of the time, Pallas kernels for 8%

profile of v4, /device:TPU:0, one launch (start us, length us, event | category | flops | bytes accessed | tf_op | source)
XLA Modules:
  0.0 44.0 jit_solution(579144344332142499)
XLA Ops:
  0.0 2.8 %shard_map.100 = f32[32,16,128]{2,1,0:T(8,128)} custom-call(f32[16,4096]{1,0:T(8,128)} %temp_hbm.1, s32[1,4096]{1,0:T(1,128)} %index_hbm.1), custom_call_target="tpu_custom_call" | custom-call | tf_op jit(solution)/shard_map/pallas_call | solution.py:228
  2.8 0.0 copy-start
  2.9 0.0 copy-start.1
  2.9 0.0 copy-start.2
  2.9 11.1 %all-to-all-start = ((f32[128,4,128]{2,1,0:T(4,128)}), f32[128,4,128]{2,1,0:T(4,128)S(1)}, u32[]{:S(2)}, u32[]{:S(2)}) async-start(f32[128,4,128]{2,1,0:T(4,128)} %bitcast), calls=%async_computation | async-start | bytes 524288 | tf_op jit(solution)/shard_map/all_to_all | solution.py:241
  14.0 4.2 %copy.13 = bf16[96,96,128]{0,1,2:T(8,128)(2,1)S(1)} copy(bf16[96,96,128]{2,1,0:T(8,128)(2,1)} %param.16) | data formatting | bytes 4718592 | tf_op args[6]
  18.2 0.0 copy-done
  18.2 0.1 copy.14
  18.3 0.1 reshape.21.connect
  18.4 0.0 copy-done.1
  18.4 0.0 copy-done.2
  18.5 6.4 %all-to-all-done = f32[128,4,128]{2,1,0:T(4,128)S(1)} async-done(((f32[128,4,128]{2,1,0:T(4,128)}), f32[128,4,128]{2,1,0:T(4,128)S(1)}, u32[]{:S(2)}, u32[]{:S(2)}) %all-to-all-start) | async-done | bytes 262176 | tf_op jit(solution)/shard_map/all_to_all | solution.py:241
  24.9 8.9 %shard_map.101 = (f32[48,4096]{1,0:T(8,128)S(1)}, f32[48,128]{1,0:T(8,128)S(1)}, f32[48,128]{1,0:T(8,128)S(1)}) custom-call(f32[32,16,128]{2,1,0:T(8,128)S(1)} %bitcast.8, s32[4,4352]{1,0:T(4,128)} %slot_hbm.1, f32[4,4352]{1,0:T(4,128)} %weight_hbm.1, bf16[48,4352]{1,0:T(8,128)(2,1)} %bitcast.10, f32[3,4352]{1,0:T(4,128)} %expansion_hbm.1, ...), custom_call_target="tpu_custom_call" | custom-call | tf_op jit(solution)/shard_map/pallas_call | solution.py:249
  33.8 0.9 %collective-permute-start = (f32[48,128]{1,0:T(8,128)S(1)}, f32[48,128]{1,0:T(8,128)S(1)}, u32[]{:S(2)}, u32[]{:S(2)}) collective-permute-start(f32[48,128]{1,0:T(8,128)S(1)} %get-tuple-element.9), channel_id=1, source_target_pairs={{0,1},{1,2},{2,3},{3,4},{4,5},{5,6},{6,7},{7,8},{8,9},{9,10},{10,1... | collective-permute-start | bytes 73736 | tf_op jit(solution)/shard_map/ppermute | solution.py:218
  34.7 4.5 %collective-permute-start.1 = (f32[48,128]{1,0:T(8,128)S(1)}, f32[48,128]{1,0:T(8,128)S(1)}, u32[]{:S(2)}, u32[]{:S(2)}) collective-permute-start(f32[48,128]{1,0:T(8,128)S(1)} %get-tuple-element.10), channel_id=1, source_target_pairs={{0,15},{1,0},{2,1},{3,2},{4,3},{5,4},{6,5},{7,6},{8,7},{9,8},{10,9... | collective-permute-start | bytes 73736 | tf_op jit(solution)/shard_map/ppermute | solution.py:218
  39.2 3.4 %shard_map.102.own = f32[48,4096]{1,0:T(8,128)S(1)} custom-call(f32[48,4096]{1,0:T(8,128)S(1)} %get-tuple-element.8.prod, s32[1,4096]{1,0:T(1,128)S(1)} %reshape.21.connect), custom_call_target="tpu_custom_call" | custom-call | tf_op jit(solution)/shard_map/pallas_call | solution.py:271
  42.7 0.0 collective-permute-done.from_lower
  42.7 0.0 collective-permute-done.1.from_upper
  42.7 1.3 %shard_map.103 = f32[48,4096]{1,0:T(8,128)} custom-call(f32[48,4096]{1,0:T(8,128)S(1)} %shard_map.102.own, f32[48,128]{1,0:T(8,128)S(1)} %collective-permute-done.from_lower, f32[48,128]{1,0:T(8,128)S(1)} %collective-permute-done.1.from_upper, s32[1,256]{1,0:T(1,128)S(1)} %bitcast.9), custom_call_target="tpu_custom_call" | custom-call | tf_op jit(solution)/shard_map/pallas_call | solution.py:272
  (2 shorter events, 0.0 us)
Async XLA Ops:
  2.8 15.4 %copy-start = (s32[32,128]{1,0:T(8,128)S(1)}, s32[32,128]{1,0:T(8,128)}, u32[]{:S(2)}) copy-start(s32[32,128]{1,0:T(8,128)} %param.17) | copy-start | bytes 49156
  2.9 15.6 %copy-start.1 = (s32[128]{0:T(128)S(1)}, s32[128]{0:T(128)}, u32[]{:S(2)}) copy-start(s32[128]{0:T(128)} %param.19) | copy-start | bytes 1540
  2.9 15.6 %copy-start.2 = (s32[128]{0:T(128)S(1)}, s32[128]{0:T(128)}, u32[]{:S(2)}) copy-start(s32[128]{0:T(128)} %param.18) | copy-start | bytes 1540
  2.9 22.0 %all-to-all-start = ((f32[128,4,128]{2,1,0:T(4,128)}), f32[128,4,128]{2,1,0:T(4,128)S(1)}, u32[]{:S(2)}, u32[]{:S(2)}) async-start(f32[128,4,128]{2,1,0:T(4,128)} %bitcast), calls=%async_computation | async-start | bytes 524288 | tf_op jit(solution)/shard_map/all_to_all | solution.py:241
  33.8 8.9 %collective-permute-start = (f32[48,128]{1,0:T(8,128)S(1)}, f32[48,128]{1,0:T(8,128)S(1)}, u32[]{:S(2)}, u32[]{:S(2)}) collective-permute-start(f32[48,128]{1,0:T(8,128)S(1)} %get-tuple-element.9), channel_id=1, source_target_pairs={{0,1},{1,2},{2,3},{3,4},{4,5},{5,6},{6,7},{7,8},{8,9},{9,10},{10,1... | collective-permute-start | bytes 73736 | tf_op jit(solution)/shard_map/ppermute | solution.py:218
  34.7 8.0 %collective-permute-start.1 = (f32[48,128]{1,0:T(8,128)S(1)}, f32[48,128]{1,0:T(8,128)S(1)}, u32[]{:S(2)}, u32[]{:S(2)}) collective-permute-start(f32[48,128]{1,0:T(8,128)S(1)} %get-tuple-element.10), channel_id=1, source_target_pairs={{0,15},{1,0},{2,1},{3,2},{4,3},{5,4},{6,5},{7,6},{8,7},{9,8},{10,9... | collective-permute-start | bytes 73736 | tf_op jit(solution)/shard_map/ppermute | solution.py:218

commit v5 on v4

--- a/solution.py
+++ b/solution.py
@@ -99,7 +99,7 @@
 
 def main_kernel(
     arrived, slot_hbm, weight_hbm, disp_hbm, expansion_hbm, blocks, connect,
-    prod, lower, upper,
+    prod, near, far,
     tab, tab3, slot, weight, disp, expansion, matrices, vec, sems,
 ):
     pairs = ((slot_hbm, slot), (weight_hbm, weight), (expansion_hbm, expansion), (disp_hbm, disp), (blocks, matrices))
@@ -173,8 +173,10 @@
     for p in range(count):
         total = ghosts(p, total)
     total = total[0:48] + total[48:96]
-    lower[...] = total[:, 0:LANES]
-    upper[...] = total[:, LANES:]
+    even = lax.rem(lax.axis_index("col"), 2) == 0
+    lower, upper = total[:, 0:LANES], total[:, LANES:]
+    near[...] = jnp.where(even, upper, lower)
+    far[...] = jnp.where(even, lower, upper)
 
 
 def turn(x, blocks):
@@ -205,17 +207,20 @@
         out[:, h * WIDE : (h + 1) * WIDE] = total[48 * h : 48 * h + 48]
 
 
-def ghost_kernel(own, from_lower, from_upper, at, out):
+def ghost_kernel(own, near, far, at, out):
     blocks = out.shape[1] // WIDE
-    total = spread(jnp.concatenate([from_lower[...], from_upper[...]], 1), at[...], blocks)
+    total = spread(jnp.concatenate([near[...], far[...]], 1), at[...], blocks)
     for h in range(blocks):
         hs = slice(h * WIDE, (h + 1) * WIDE)
         out[:, hs] = own[:, hs] + total[48 * h : 48 * h + 48]
 
 
-def neighbour(block, distance):
+def swap(block, first):
     count = lax.axis_size("col")
-    return lax.ppermute(block, "col", [(i, (i + distance) % count) for i in range(count)])
+    partner = list(range(count))
+    for i in range(first, count - 1, 2):
+        partner[i], partner[i + 1] = i + 1, i
+    return lax.ppermute(block, "col", list(enumerate(partner)))
 
 
 def shards(temp_thermal, send_index, interp_slot, interp_weight, disp, expansion, tangent, connect, recv_lower, recv_upper):
@@ -243,10 +248,15 @@
     links = connect.T.reshape(1, 4096)
     blocks = jnp.transpose(tangent, (2, 1, 0))
     col = lax.axis_index("col")
+    even = col % 2 == 0
+    edge = (col == 0) | (col == lax.axis_size("col") - 1)
     at = jnp.concatenate(
-        [jnp.where(col > 0, recv_lower, -1), jnp.where(col < lax.axis_size("col") - 1, recv_upper, -1)]
+        [
+            jnp.where(even, recv_upper, recv_lower),
+            jnp.where(edge, -1, jnp.where(even, recv_lower, recv_upper)),
+        ]
     ).reshape(1, WIDE)
-    prod, lower, upper = pl.pallas_call(
+    prod, near, far = pl.pallas_call(
         main_kernel,
         out_shape=(shape((48, 4096), F32), shape((48, LANES), F32), shape((48, LANES), F32)),
         in_specs=[here, away, away, away, away, free, here],
@@ -266,11 +276,11 @@
     )(
         arrived, keep(interp_slot), keep(interp_weight), keep(disp.reshape(48, -1)), keep(expansion), blocks, links
     )
-    from_lower = neighbour(upper, 1)
-    from_upper = neighbour(lower, -1)
+    got_far = swap(far, 1)
+    got_near = swap(near, 0)
     own = pl.pallas_call(owned_kernel, out_shape=shape((48, 4096), F32), compiler_params=params)(prod, links)
     result = pl.pallas_call(ghost_kernel, out_shape=shape((48, 4096), F32), compiler_params=params)(
-        own, from_lower, from_upper, at
+        own, got_near, got_far, at
     )
     return result.reshape(3, 16, 4096)
 

time: 44.3 us -> 43.2 us (0.975)
  the two profiles are of different devices: /device:TPU:0 before, /device:TPU:2 now
where the time goes in v5:
time: 43.2 us; the launch traced here: 42.8 us
  Pallas kernels  16.4 us (38%)
  starting transfers between devices  14.7 us (34%)
  waiting for transfers between devices  7.14 us (17%)
  local copies, waits for them, and re-layouts  4.39 us (10%)
    all_to_all x1, starting transfers between devices, shards(): lax.all_to_all(packed.reshape(128, 4, LANES), AXES, split_axis=0, concat_...  10.5 us
    pallas_call x1, Pallas kernels, shards(): pl.pallas_call(main_kernel, out_shape=(shape((48, 4096), F32), shape((48,...  8.88 us
    all_to_all x1, waiting for transfers between devices, shards(): lax.all_to_all(packed.reshape(128, 4, LANES), AXES, split_axis=0, concat_...  6.04 us
    unnamed x7, local copies, waits for them, and re-layouts  4.2 us
    ppermute x2, starting transfers between devices, swap(): return lax.ppermute(block, 'col', list(enumerate(partner)))  4.17 us
    pallas_call x1, Pallas kernels, shards(): pl.pallas_call(owned_kernel, out_shape=shape((48, 4096), F32), compiler_p...  3.44 us
    pallas_call x1, Pallas kernels, shards(): pl.pallas_call(send_kernel, out_shape=shape((32, 16, LANES), F32), in_spe...  2.84 us
    pallas_call x1, Pallas kernels, shards(): pl.pallas_call(ghost_kernel, out_shape=shape((48, 4096), F32), compiler_p...  1.29 us
  transfers between devices with their start and end apart: 3, of which 2 were waited for; matrix products, arithmetic and copies ran while one was open for 10% of the time, Pallas kernels for 8%

profile of v5, /device:TPU:2, one launch (start us, length us, event | category | flops | bytes accessed | tf_op | source)
XLA Modules:
  0.0 42.8 jit_solution(14395615872320643418)
XLA Ops:
  0.0 2.8 %shard_map.100 = f32[32,16,128]{2,1,0:T(8,128)} custom-call(f32[16,4096]{1,0:T(8,128)} %temp_hbm.1, s32[1,4096]{1,0:T(1,128)} %index_hbm.1), custom_call_target="tpu_custom_call" | custom-call | tf_op jit(solution)/shard_map/pallas_call | solution.py:233
  2.8 0.0 copy-start
  2.9 0.0 copy-start.1
  2.9 0.0 copy-start.2
  2.9 10.5 %all-to-all-start = ((f32[128,4,128]{2,1,0:T(4,128)}), f32[128,4,128]{2,1,0:T(4,128)S(1)}, u32[]{:S(2)}, u32[]{:S(2)}) async-start(f32[128,4,128]{2,1,0:T(4,128)} %bitcast), calls=%async_computation | async-start | bytes 524288 | tf_op jit(solution)/shard_map/all_to_all | solution.py:246
  13.4 4.2 %copy.13 = bf16[96,96,128]{0,1,2:T(8,128)(2,1)S(1)} copy(bf16[96,96,128]{2,1,0:T(8,128)(2,1)} %param.16) | data formatting | bytes 4718592 | tf_op args[6]
  17.6 0.0 copy-done
  17.6 0.1 copy.14
  17.7 0.1 reshape.21.connect
  17.8 0.0 copy-done.1
  17.9 0.0 copy-done.2
  17.9 6.0 %all-to-all-done = f32[128,4,128]{2,1,0:T(4,128)S(1)} async-done(((f32[128,4,128]{2,1,0:T(4,128)}), f32[128,4,128]{2,1,0:T(4,128)S(1)}, u32[]{:S(2)}, u32[]{:S(2)}) %all-to-all-start) | async-done | bytes 262176 | tf_op jit(solution)/shard_map/all_to_all | solution.py:246
  23.9 8.9 %shard_map.101 = (f32[48,4096]{1,0:T(8,128)S(1)}, f32[48,128]{1,0:T(8,128)S(1)}, f32[48,128]{1,0:T(8,128)S(1)}) custom-call(f32[32,16,128]{2,1,0:T(8,128)S(1)} %bitcast.8, s32[4,4352]{1,0:T(4,128)} %slot_hbm.1, f32[4,4352]{1,0:T(4,128)} %weight_hbm.1, bf16[48,4352]{1,0:T(8,128)(2,1)} %bitcast.10, f32[3,4352]{1,0:T(4,128)} %expansion_hbm.1, ...), custom_call_target="tpu_custom_call" | custom-call | tf_op jit(solution)/shard_map/pallas_call | solution.py:259
  32.8 0.9 %collective-permute-start = (f32[48,128]{1,0:T(8,128)S(1)}, f32[48,128]{1,0:T(8,128)S(1)}, u32[]{:S(2)}, u32[]{:S(2)}) collective-permute-start(f32[48,128]{1,0:T(8,128)S(1)} %get-tuple-element.9), channel_id=1, source_target_pairs={{0,1},{1,0},{2,3},{3,2},{4,5},{5,4},{6,7},{7,6},{8,9},{9,8},{10,11... | collective-permute-start | bytes 73736 | tf_op jit(solution)/shard_map/ppermute | solution.py:223
  33.7 3.2 %collective-permute-start.1 = (f32[48,128]{1,0:T(8,128)S(1)}, f32[48,128]{1,0:T(8,128)S(1)}, u32[]{:S(2)}, u32[]{:S(2)}) collective-permute-start(f32[48,128]{1,0:T(8,128)S(1)} %get-tuple-element.10), channel_id=1, source_target_pairs={{0,0},{1,2},{2,1},{3,4},{4,3},{5,6},{6,5},{7,8},{8,7},{9,10},{10,9... | collective-permute-start | bytes 73736 | tf_op jit(solution)/shard_map/ppermute | solution.py:223
  37.0 3.4 %shard_map.102.own = f32[48,4096]{1,0:T(8,128)S(1)} custom-call(f32[48,4096]{1,0:T(8,128)S(1)} %get-tuple-element.8.prod, s32[1,4096]{1,0:T(1,128)S(1)} %reshape.21.connect), custom_call_target="tpu_custom_call" | custom-call | tf_op jit(solution)/shard_map/pallas_call | solution.py:281
  40.4 0.0 collective-permute-done.near
  40.5 1.1 %collective-permute-done.1.far = f32[48,128]{1,0:T(8,128)S(1)} collective-permute-done((f32[48,128]{1,0:T(8,128)S(1)}, f32[48,128]{1,0:T(8,128)S(1)}, u32[]{:S(2)}, u32[]{:S(2)}) %collective-permute-start.1) | collective-permute-done | bytes 24608 | tf_op jit(solution)/shard_map/ppermute | solution.py:223
  41.6 1.3 %shard_map.103 = f32[48,4096]{1,0:T(8,128)} custom-call(f32[48,4096]{1,0:T(8,128)S(1)} %shard_map.102.own, f32[48,128]{1,0:T(8,128)S(1)} %collective-permute-done.near, f32[48,128]{1,0:T(8,128)S(1)} %collective-permute-done.1.far, s32[1,256]{1,0:T(1,128)S(1)} %bitcast.9), custom_call_target="tpu_custom_call" | custom-call | tf_op jit(solution)/shard_map/pallas_call | solution.py:282
  (2 shorter events, 0.0 us)
Async XLA Ops:
  2.8 14.8 %copy-start = (s32[32,128]{1,0:T(8,128)S(1)}, s32[32,128]{1,0:T(8,128)}, u32[]{:S(2)}) copy-start(s32[32,128]{1,0:T(8,128)} %param.17) | copy-start | bytes 49156
  2.9 15.0 %copy-start.1 = (s32[128]{0:T(128)S(1)}, s32[128]{0:T(128)}, u32[]{:S(2)}) copy-start(s32[128]{0:T(128)} %param.19) | copy-start | bytes 1540
  2.9 15.0 %copy-start.2 = (s32[128]{0:T(128)S(1)}, s32[128]{0:T(128)}, u32[]{:S(2)}) copy-start(s32[128]{0:T(128)} %param.18) | copy-start | bytes 1540
  2.9 21.0 %all-to-all-start = ((f32[128,4,128]{2,1,0:T(4,128)}), f32[128,4,128]{2,1,0:T(4,128)S(1)}, u32[]{:S(2)}, u32[]{:S(2)}) async-start(f32[128,4,128]{2,1,0:T(4,128)} %bitcast), calls=%async_computation | async-start | bytes 524288 | tf_op jit(solution)/shard_map/all_to_all | solution.py:246
  32.8 7.6 %collective-permute-start = (f32[48,128]{1,0:T(8,128)S(1)}, f32[48,128]{1,0:T(8,128)S(1)}, u32[]{:S(2)}, u32[]{:S(2)}) collective-permute-start(f32[48,128]{1,0:T(8,128)S(1)} %get-tuple-element.9), channel_id=1, source_target_pairs={{0,1},{1,0},{2,3},{3,2},{4,5},{5,4},{6,7},{7,6},{8,9},{9,8},{10,11... | collective-permute-start | bytes 73736 | tf_op jit(solution)/shard_map/ppermute | solution.py:223
  33.7 7.8 %collective-permute-start.1 = (f32[48,128]{1,0:T(8,128)S(1)}, f32[48,128]{1,0:T(8,128)S(1)}, u32[]{:S(2)}, u32[]{:S(2)}) collective-permute-start(f32[48,128]{1,0:T(8,128)S(1)} %get-tuple-element.10), channel_id=1, source_target_pairs={{0,0},{1,2},{2,1},{3,4},{4,3},{5,6},{6,5},{7,8},{8,7},{9,10},{10,9... | collective-permute-start | bytes 73736 | tf_op jit(solution)/shard_map/ppermute | solution.py:223

commit v6 on v5

--- a/solution.py
+++ b/solution.py
@@ -8,6 +8,8 @@
 F32 = jnp.float32
 BF16 = jnp.bfloat16
 I32 = jnp.int32
+FINE = jnp.float8_e5m2
+RAISE = 4096.0
 LANES = 128
 WIDE = 256
 AXES = ("row", "col")
@@ -196,15 +198,33 @@
     )
 
 
+def spread_parts(x, idx, blocks):
+    zero = jnp.zeros((), BF16)
+    hot = one_hot(idx & (WIDE - 1), iota_of(WIDE))
+    high = jnp.broadcast_to((idx >> 8).astype(F32).astype(BF16), x.shape)
+    first = x.astype(BF16)
+    second = ((x - first.astype(F32)) * RAISE).astype(BF16)
+    first, second = (
+        jnp.concatenate([jnp.where(high == jnp.array(h, BF16), part, zero) for h in range(blocks)], 0)
+        for part in (first, second)
+    )
+    return (
+        lax.dot_general(first, hot, NT, preferred_element_type=F32),
+        lax.dot_general(second.astype(FINE), hot.astype(FINE), NT, preferred_element_type=F32),
+    )
+
+
 def owned_kernel(prod, connect, out):
     blocks = out.shape[1] // WIDE
-    total = None
+    first = second = None
     for p in range(connect.shape[1] // WIDE):
         ks = slice(p * WIDE, (p + 1) * WIDE)
-        term = spread(prod[:, ks], connect[0:1, ks], blocks)
-        total = term if total is None else total + term
+        x, y = spread_parts(prod[:, ks], connect[0:1, ks], blocks)
+        first = x if first is None else first + x
+        second = y if second is None else second + y
     for h in range(blocks):
-        out[:, h * WIDE : (h + 1) * WIDE] = total[48 * h : 48 * h + 48]
+        rows = slice(48 * h, 48 * h + 48)
+        out[:, h * WIDE : (h + 1) * WIDE] = first[rows] + second[rows] * (1.0 / RAISE)
 
 
 def ghost_kernel(own, near, far, at, out):

time: 43.2 us -> 43.2 us (level)
  waiting for transfers between devices: 7.14 us -> 7.89 us
  Pallas kernels: 16.4 us -> 15.7 us
    pallas_call x1, Pallas kernels: 3.44 us -> 2.69 us  [shards(): pl.pallas_call(owned_kernel, out_shape=shape((48, 4096), F32), compiler_p...]
    ppermute x2, waiting for transfers between devices: 1.1 us -> 1.85 us  [swap(): return lax.ppermute(block, 'col', list(enumerate(partner)))]
  transfers between devices with their start and end apart: 3 -> 3, of which waited for: 2 -> 2; matrix products, arithmetic and copies ran while one was open for 10% -> 10% of each run, Pallas kernels for 8% -> 6%
where the time goes in v6:
time: 43.2 us; the launch traced here: 42.8 us
  Pallas kernels  15.7 us (36%)
  starting transfers between devices  14.7 us (34%)
  waiting for transfers between devices  7.89 us (18%)
  local copies, waits for them, and re-layouts  4.39 us (10%)
    all_to_all x1, starting transfers between devices, shards(): lax.all_to_all(packed.reshape(128, 4, LANES), AXES, split_axis=0, concat_...  10.5 us
    pallas_call x1, Pallas kernels, shards(): pl.pallas_call(main_kernel, out_shape=(shape((48, 4096), F32), shape((48,...  8.88 us
    all_to_all x1, waiting for transfers between devices, shards(): lax.all_to_all(packed.reshape(128, 4, LANES), AXES, split_axis=0, concat_...  6.04 us
    unnamed x7, local copies, waits for them, and re-layouts  4.2 us
    ppermute x2, starting transfers between devices, swap(): return lax.ppermute(block, 'col', list(enumerate(partner)))  4.17 us
    pallas_call x1, Pallas kernels, shards(): pl.pallas_call(send_kernel, out_shape=shape((32, 16, LANES), F32), in_spe...  2.84 us
    pallas_call x1, Pallas kernels, shards(): pl.pallas_call(owned_kernel, out_shape=shape((48, 4096), F32), compiler_p...  2.69 us
    ppermute x2, waiting for transfers between devices, swap(): return lax.ppermute(block, 'col', list(enumerate(partner)))  1.85 us
  transfers between devices with their start and end apart: 3, of which 2 were waited for; matrix products, arithmetic and copies ran while one was open for 10% of the time, Pallas kernels for 6%

profile of v6, /device:TPU:2, one launch (start us, length us, event | category | flops | bytes accessed | tf_op | source)
XLA Modules:
  0.0 42.8 jit_solution(9070867286321272407)
XLA Ops:
  0.0 2.8 %shard_map.100 = f32[32,16,128]{2,1,0:T(8,128)} custom-call(f32[16,4096]{1,0:T(8,128)} %temp_hbm.1, s32[1,4096]{1,0:T(1,128)} %index_hbm.1), custom_call_target="tpu_custom_call" | custom-call | tf_op jit(solution)/shard_map/pallas_call | solution.py:253
  2.8 0.0 copy-start
  2.9 0.0 copy-start.1
  2.9 0.0 copy-start.2
  2.9 10.5 %all-to-all-start = ((f32[128,4,128]{2,1,0:T(4,128)}), f32[128,4,128]{2,1,0:T(4,128)S(1)}, u32[]{:S(2)}, u32[]{:S(2)}) async-start(f32[128,4,128]{2,1,0:T(4,128)} %bitcast), calls=%async_computation | async-start | bytes 524288 | tf_op jit(solution)/shard_map/all_to_all | solution.py:266
  13.4 4.2 %copy.13 = bf16[96,96,128]{0,1,2:T(8,128)(2,1)S(1)} copy(bf16[96,96,128]{2,1,0:T(8,128)(2,1)} %param.16) | data formatting | bytes 4718592 | tf_op args[6]
  17.6 0.0 copy-done
  17.6 0.1 copy.14
  17.7 0.1 reshape.21.connect
  17.8 0.0 copy-done.1
  17.9 0.0 copy-done.2
  17.9 6.0 %all-to-all-done = f32[128,4,128]{2,1,0:T(4,128)S(1)} async-done(((f32[128,4,128]{2,1,0:T(4,128)}), f32[128,4,128]{2,1,0:T(4,128)S(1)}, u32[]{:S(2)}, u32[]{:S(2)}) %all-to-all-start) | async-done | bytes 262176 | tf_op jit(solution)/shard_map/all_to_all | solution.py:266
  23.9 8.9 %shard_map.101 = (f32[48,4096]{1,0:T(8,128)S(1)}, f32[48,128]{1,0:T(8,128)S(1)}, f32[48,128]{1,0:T(8,128)S(1)}) custom-call(f32[32,16,128]{2,1,0:T(8,128)S(1)} %bitcast.8, s32[4,4352]{1,0:T(4,128)} %slot_hbm.1, f32[4,4352]{1,0:T(4,128)} %weight_hbm.1, bf16[48,4352]{1,0:T(8,128)(2,1)} %bitcast.10, f32[3,4352]{1,0:T(4,128)} %expansion_hbm.1, ...), custom_call_target="tpu_custom_call" | custom-call | tf_op jit(solution)/shard_map/pallas_call | solution.py:279
  32.8 0.9 %collective-permute-start = (f32[48,128]{1,0:T(8,128)S(1)}, f32[48,128]{1,0:T(8,128)S(1)}, u32[]{:S(2)}, u32[]{:S(2)}) collective-permute-start(f32[48,128]{1,0:T(8,128)S(1)} %get-tuple-element.9), channel_id=1, source_target_pairs={{0,1},{1,0},{2,3},{3,2},{4,5},{5,4},{6,7},{7,6},{8,9},{9,8},{10,11... | collective-permute-start | bytes 73736 | tf_op jit(solution)/shard_map/ppermute | solution.py:243
  33.7 3.2 %collective-permute-start.1 = (f32[48,128]{1,0:T(8,128)S(1)}, f32[48,128]{1,0:T(8,128)S(1)}, u32[]{:S(2)}, u32[]{:S(2)}) collective-permute-start(f32[48,128]{1,0:T(8,128)S(1)} %get-tuple-element.10), channel_id=1, source_target_pairs={{0,0},{1,2},{2,1},{3,4},{4,3},{5,6},{6,5},{7,8},{8,7},{9,10},{10,9... | collective-permute-start | bytes 73736 | tf_op jit(solution)/shard_map/ppermute | solution.py:243
  37.0 2.7 %shard_map.102.own = f32[48,4096]{1,0:T(8,128)S(1)} custom-call(f32[48,4096]{1,0:T(8,128)S(1)} %get-tuple-element.8.prod, s32[1,4096]{1,0:T(1,128)S(1)} %reshape.21.connect), custom_call_target="tpu_custom_call" | custom-call | tf_op jit(solution)/shard_map/pallas_call | solution.py:301
  39.7 0.0 collective-permute-done.near
  39.7 1.8 %collective-permute-done.1.far = f32[48,128]{1,0:T(8,128)S(1)} collective-permute-done((f32[48,128]{1,0:T(8,128)S(1)}, f32[48,128]{1,0:T(8,128)S(1)}, u32[]{:S(2)}, u32[]{:S(2)}) %collective-permute-start.1) | collective-permute-done | bytes 24608 | tf_op jit(solution)/shard_map/ppermute | solution.py:243
  41.6 1.3 %shard_map.103 = f32[48,4096]{1,0:T(8,128)} custom-call(f32[48,4096]{1,0:T(8,128)S(1)} %shard_map.102.own, f32[48,128]{1,0:T(8,128)S(1)} %collective-permute-done.near, f32[48,128]{1,0:T(8,128)S(1)} %collective-permute-done.1.far, s32[1,256]{1,0:T(1,128)S(1)} %bitcast.9), custom_call_target="tpu_custom_call" | custom-call | tf_op jit(solution)/shard_map/pallas_call | solution.py:302
  (2 shorter events, 0.0 us)
Async XLA Ops:
  2.8 14.8 %copy-start = (s32[32,128]{1,0:T(8,128)S(1)}, s32[32,128]{1,0:T(8,128)}, u32[]{:S(2)}) copy-start(s32[32,128]{1,0:T(8,128)} %param.17) | copy-start | bytes 49156
  2.9 15.0 %copy-start.1 = (s32[128]{0:T(128)S(1)}, s32[128]{0:T(128)}, u32[]{:S(2)}) copy-start(s32[128]{0:T(128)} %param.19) | copy-start | bytes 1540
  2.9 15.0 %copy-start.2 = (s32[128]{0:T(128)S(1)}, s32[128]{0:T(128)}, u32[]{:S(2)}) copy-start(s32[128]{0:T(128)} %param.18) | copy-start | bytes 1540
  2.9 21.0 %all-to-all-start = ((f32[128,4,128]{2,1,0:T(4,128)}), f32[128,4,128]{2,1,0:T(4,128)S(1)}, u32[]{:S(2)}, u32[]{:S(2)}) async-start(f32[128,4,128]{2,1,0:T(4,128)} %bitcast), calls=%async_computation | async-start | bytes 524288 | tf_op jit(solution)/shard_map/all_to_all | solution.py:266
  32.8 6.9 %collective-permute-start = (f32[48,128]{1,0:T(8,128)S(1)}, f32[48,128]{1,0:T(8,128)S(1)}, u32[]{:S(2)}, u32[]{:S(2)}) collective-permute-start(f32[48,128]{1,0:T(8,128)S(1)} %get-tuple-element.9), channel_id=1, source_target_pairs={{0,1},{1,0},{2,3},{3,2},{4,5},{5,4},{6,7},{7,6},{8,9},{9,8},{10,11... | collective-permute-start | bytes 73736 | tf_op jit(solution)/shard_map/ppermute | solution.py:243
  33.7 7.8 %collective-permute-start.1 = (f32[48,128]{1,0:T(8,128)S(1)}, f32[48,128]{1,0:T(8,128)S(1)}, u32[]{:S(2)}, u32[]{:S(2)}) collective-permute-start(f32[48,128]{1,0:T(8,128)S(1)} %get-tuple-element.10), channel_id=1, source_target_pairs={{0,0},{1,2},{2,1},{3,4},{4,3},{5,6},{6,5},{7,8},{8,7},{9,10},{10,9... | collective-permute-start | bytes 73736 | tf_op jit(solution)/shard_map/ppermute | solution.py:243

commit v7 on v6

--- a/solution.py
+++ b/solution.py
@@ -8,6 +8,8 @@
 F32 = jnp.float32
 BF16 = jnp.bfloat16
 I32 = jnp.int32
+SHORT = jnp.float8_e4m3fn
+TOP = 384.0
 FINE = jnp.float8_e5m2
 RAISE = 4096.0
 LANES = 128
@@ -110,9 +112,17 @@
         copy.start()
     extent = slot.shape[1]
 
+    largest = jnp.max(jnp.abs(arrived[...]), axis=0)
+    largest = jnp.max(jnp.max(largest, axis=1, keepdims=True), axis=0, keepdims=True)
+    largest = jnp.where(largest > 0.0, largest, 1.0)
+    back = largest * (1.0 / TOP)
+    raise_by = TOP / largest
     for h in range(0, arrived.shape[0] // 2, 2):
-        tiles = [swap_blocks(arrived[2 * h + i]) for i in range(4)]
-        fill_pair(tab, h, jnp.concatenate(tiles[0:2], 1), jnp.concatenate(tiles[2:4], 1))
+        tiles = [swap_blocks(arrived[2 * h + i]) * raise_by for i in range(4)]
+        block = jnp.concatenate([jnp.concatenate(tiles[0:2], 1), jnp.concatenate(tiles[2:4], 1)], 0)
+        first = block.astype(SHORT)
+        tab[16 * h : 16 * h + 32, 0:WIDE] = first
+        tab[16 * h : 16 * h + 32, WIDE : 2 * WIDE] = (block - first.astype(F32)).astype(SHORT)
     iota = iota_of(WIDE)
     for copy in copies[0:4]:
         copy.wait()
@@ -123,7 +133,10 @@
         for c in range(4):
             idx = slot[c : c + 1, js]
             hot = one_hot(idx & (WIDE - 1), iota)
-            temp = temp + weight[c : c + 1, js] * look_up(tab, hot, idx >> 8)
+            hot = hot.astype(SHORT)
+            stacked = jnp.dot(tab[...], jnp.concatenate([hot, hot], 0), preferred_element_type=F32)
+            temp = temp + weight[c : c + 1, js] * choose(stacked, idx >> 8, 16)
+        temp = temp * back
         strain = temp / jnp.sqrt(1.0 + temp * temp)
         for a in range(3):
             d = disp[16 * a : 16 * a + 16, js].astype(F32)
@@ -227,7 +240,7 @@
         out[:, h * WIDE : (h + 1) * WIDE] = first[rows] + second[rows] * (1.0 / RAISE)
 
 
-def ghost_kernel(own, near, far, at, out):
+def ghost_kernel(far, near, own, at, out):
     blocks = out.shape[1] // WIDE
     total = spread(jnp.concatenate([near[...], far[...]], 1), at[...], blocks)
     for h in range(blocks):
@@ -282,7 +295,7 @@
         in_specs=[here, away, away, away, away, free, here],
         out_specs=(here, here, here),
         scratch_shapes=[
-            pltpu.VMEM((384, WIDE), BF16),
+            pltpu.VMEM((256, 2 * WIDE), SHORT),
             pltpu.VMEM((17 * 48, WIDE), BF16),
             pltpu.VMEM((4, 4352), I32),
             pltpu.VMEM((4, 4352), F32),
@@ -300,7 +313,7 @@
     got_near = swap(near, 0)
     own = pl.pallas_call(owned_kernel, out_shape=shape((48, 4096), F32), compiler_params=params)(prod, links)
     result = pl.pallas_call(ghost_kernel, out_shape=shape((48, 4096), F32), compiler_params=params)(
-        own, got_near, got_far, at
+        got_far, got_near, own, at
     )
     return result.reshape(3, 16, 4096)
 

time: 43.2 us -> 41.1 us (0.951)
  Pallas kernels: 15.7 us -> 14.5 us
  starting transfers between devices: 14.7 us -> 14 us
    pallas_call x1, Pallas kernels: 8.88 us -> 7.7 us  [shards(): pl.pallas_call(main_kernel, out_shape=(shape((48, 4096), F32), shape((48,...]
    ppermute x2, starting transfers between devices: 4.17 us -> 3.52 us  [swap(): return lax.ppermute(block, 'col', list(enumerate(partner)))]
  transfers between devices with their start and end apart: 3 -> 3, of which waited for: 2 -> 2; matrix products, arithmetic and copies ran while one was open for 10% -> 11% of each run, Pallas kernels for 6% -> 7%
where the time goes in v7:
time: 41.1 us; the launch traced here: 40.8 us
  Pallas kernels  14.5 us (35%)
  starting transfers between devices  14 us (34%)
  waiting for transfers between devices  7.62 us (19%)
  local copies, waits for them, and re-layouts  4.39 us (11%)
    all_to_all x1, starting transfers between devices, shards(): lax.all_to_all(packed.reshape(128, 4, LANES), AXES, split_axis=0, concat_...  10.5 us
    pallas_call x1, Pallas kernels, shards(): pl.pallas_call(main_kernel, out_shape=(shape((48, 4096), F32), shape((48,...  7.7 us
    all_to_all x1, waiting for transfers between devices, shards(): lax.all_to_all(packed.reshape(128, 4, LANES), AXES, split_axis=0, concat_...  6.04 us
    unnamed x7, local copies, waits for them, and re-layouts  4.2 us
    ppermute x2, starting transfers between devices, swap(): return lax.ppermute(block, 'col', list(enumerate(partner)))  3.52 us
    pallas_call x1, Pallas kernels, shards(): pl.pallas_call(send_kernel, out_shape=shape((32, 16, LANES), F32), in_spe...  2.84 us
    pallas_call x1, Pallas kernels, shards(): pl.pallas_call(owned_kernel, out_shape=shape((48, 4096), F32), compiler_p...  2.69 us
    ppermute x2, waiting for transfers between devices, swap(): return lax.ppermute(block, 'col', list(enumerate(partner)))  1.59 us
  transfers between devices with their start and end apart: 3, of which 2 were waited for; matrix products, arithmetic and copies ran while one was open for 11% of the time, Pallas kernels for 7%

profile of v7, /device:TPU:2, one launch (start us, length us, event | category | flops | bytes accessed | tf_op | source)
XLA Modules:
  0.0 40.8 jit_solution(16305532111222964227)
XLA Ops:
  0.0 2.8 %shard_map.100 = f32[32,16,128]{2,1,0:T(8,128)} custom-call(f32[16,4096]{1,0:T(8,128)} %temp_hbm.1, s32[1,4096]{1,0:T(1,128)} %index_hbm.1), custom_call_target="tpu_custom_call" | custom-call | tf_op jit(solution)/shard_map/pallas_call | solution.py:266
  2.8 0.0 copy-start
  2.9 0.0 copy-start.1
  2.9 0.0 copy-start.2
  2.9 10.5 %all-to-all-start = ((f32[128,4,128]{2,1,0:T(4,128)}), f32[128,4,128]{2,1,0:T(4,128)S(1)}, u32[]{:S(2)}, u32[]{:S(2)}) async-start(f32[128,4,128]{2,1,0:T(4,128)} %bitcast), calls=%async_computation | async-start | bytes 524288 | tf_op jit(solution)/shard_map/all_to_all | solution.py:279
  13.4 4.2 %copy.13 = bf16[96,96,128]{0,1,2:T(8,128)(2,1)S(1)} copy(bf16[96,96,128]{2,1,0:T(8,128)(2,1)} %param.16) | data formatting | bytes 4718592 | tf_op args[6]
  17.6 0.0 copy-done
  17.6 0.1 copy.14
  17.7 0.1 reshape.21.connect
  17.8 0.0 copy-done.1
  17.9 0.0 copy-done.2
  17.9 6.0 %all-to-all-done = f32[128,4,128]{2,1,0:T(4,128)S(1)} async-done(((f32[128,4,128]{2,1,0:T(4,128)}), f32[128,4,128]{2,1,0:T(4,128)S(1)}, u32[]{:S(2)}, u32[]{:S(2)}) %all-to-all-start) | async-done | bytes 262176 | tf_op jit(solution)/shard_map/all_to_all | solution.py:279
  23.9 7.7 %shard_map.101 = (f32[48,4096]{1,0:T(8,128)S(1)}, f32[48,128]{1,0:T(8,128)S(1)}, f32[48,128]{1,0:T(8,128)S(1)}) custom-call(f32[32,16,128]{2,1,0:T(8,128)S(1)} %bitcast.8, s32[4,4352]{1,0:T(4,128)} %slot_hbm.1, f32[4,4352]{1,0:T(4,128)} %weight_hbm.1, bf16[48,4352]{1,0:T(8,128)(2,1)} %bitcast.10, f32[3,4352]{1,0:T(4,128)} %expansion_hbm.1, ...), custom_call_target="tpu_custom_call" | custom-call | tf_op jit(solution)/shard_map/pallas_call | solution.py:292
  31.6 3.3 %collective-permute-start = (f32[48,128]{1,0:T(8,128)S(1)}, f32[48,128]{1,0:T(8,128)S(1)}, u32[]{:S(2)}, u32[]{:S(2)}) collective-permute-start(f32[48,128]{1,0:T(8,128)S(1)} %get-tuple-element.8), channel_id=1, source_target_pairs={{0,0},{1,2},{2,1},{3,4},{4,3},{5,6},{6,5},{7,8},{8,7},{9,10},{10,9... | collective-permute-start | bytes 73736 | tf_op jit(solution)/shard_map/ppermute | solution.py:256
  34.9 0.3 collective-permute-start.1
  35.2 2.7 %shard_map.102.own = f32[48,4096]{1,0:T(8,128)S(1)} custom-call(f32[48,4096]{1,0:T(8,128)S(1)} %get-tuple-element.10.prod, s32[1,4096]{1,0:T(1,128)S(1)} %reshape.21.connect), custom_call_target="tpu_custom_call" | custom-call | tf_op jit(solution)/shard_map/pallas_call | solution.py:314
  37.9 1.6 %collective-permute-done.far = f32[48,128]{1,0:T(8,128)S(1)} collective-permute-done((f32[48,128]{1,0:T(8,128)S(1)}, f32[48,128]{1,0:T(8,128)S(1)}, u32[]{:S(2)}, u32[]{:S(2)}) %collective-permute-start) | collective-permute-done | bytes 24608 | tf_op jit(solution)/shard_map/ppermute | solution.py:256
  39.5 0.0 collective-permute-done.1.near
  39.5 1.3 %shard_map.103 = f32[48,4096]{1,0:T(8,128)} custom-call(f32[48,128]{1,0:T(8,128)S(1)} %collective-permute-done.far, f32[48,128]{1,0:T(8,128)S(1)} %collective-permute-done.1.near, f32[48,4096]{1,0:T(8,128)S(1)} %shard_map.102.own, s32[1,256]{1,0:T(1,128)S(1)} %bitcast.9), custom_call_target="tpu_custom_call" | custom-call | tf_op jit(solution)/shard_map/pallas_call | solution.py:315
  (2 shorter events, 0.0 us)
Async XLA Ops:
  2.8 14.8 %copy-start = (s32[32,128]{1,0:T(8,128)S(1)}, s32[32,128]{1,0:T(8,128)}, u32[]{:S(2)}) copy-start(s32[32,128]{1,0:T(8,128)} %param.17) | copy-start | bytes 49156
  2.9 15.0 %copy-start.1 = (s32[128]{0:T(128)S(1)}, s32[128]{0:T(128)}, u32[]{:S(2)}) copy-start(s32[128]{0:T(128)} %param.19) | copy-start | bytes 1540
  2.9 15.0 %copy-start.2 = (s32[128]{0:T(128)S(1)}, s32[128]{0:T(128)}, u32[]{:S(2)}) copy-start(s32[128]{0:T(128)} %param.18) | copy-start | bytes 1540
  2.9 21.0 %all-to-all-start = ((f32[128,4,128]{2,1,0:T(4,128)}), f32[128,4,128]{2,1,0:T(4,128)S(1)}, u32[]{:S(2)}, u32[]{:S(2)}) async-start(f32[128,4,128]{2,1,0:T(4,128)} %bitcast), calls=%async_computation | async-start | bytes 524288 | tf_op jit(solution)/shard_map/all_to_all | solution.py:279
  31.6 7.8 %collective-permute-start = (f32[48,128]{1,0:T(8,128)S(1)}, f32[48,128]{1,0:T(8,128)S(1)}, u32[]{:S(2)}, u32[]{:S(2)}) collective-permute-start(f32[48,128]{1,0:T(8,128)S(1)} %get-tuple-element.8), channel_id=1, source_target_pairs={{0,0},{1,2},{2,1},{3,4},{4,3},{5,6},{6,5},{7,8},{8,7},{9,10},{10,9... | collective-permute-start | bytes 73736 | tf_op jit(solution)/shard_map/ppermute | solution.py:256
  34.9 4.6 %collective-permute-start.1 = (f32[48,128]{1,0:T(8,128)S(1)}, f32[48,128]{1,0:T(8,128)S(1)}, u32[]{:S(2)}, u32[]{:S(2)}) collective-permute-start(f32[48,128]{1,0:T(8,128)S(1)} %get-tuple-element.9), channel_id=1, source_target_pairs={{0,1},{1,0},{2,3},{3,2},{4,5},{5,4},{6,7},{7,6},{8,9},{9,8},{10,11... | collective-permute-start | bytes 73736 | tf_op jit(solution)/shard_map/ppermute | solution.py:256

commit v8 on v6

--- a/solution.py
+++ b/solution.py
@@ -8,6 +8,8 @@
 F32 = jnp.float32
 BF16 = jnp.bfloat16
 I32 = jnp.int32
+SHORT = jnp.float8_e4m3fn
+TOP = 384.0
 FINE = jnp.float8_e5m2
 RAISE = 4096.0
 LANES = 128
@@ -99,22 +101,66 @@
         out[2 * j + 1] = swap_blocks(got[:, LANES:])
 
 
+def pick_kernel(disp_hbm, expansion_hbm, connect, picked, factor, disp, expansion, both, tab, sems):
+    copies = [
+        pltpu.make_async_copy(disp_hbm, disp, sems.at[0]),
+        pltpu.make_async_copy(expansion_hbm, expansion, sems.at[1]),
+    ]
+    for copy in copies:
+        copy.start()
+    for copy in copies:
+        copy.wait()
+    blocks = disp.shape[1] // WIDE
+    base = 48 * blocks
+    high, low = split(expansion[...])
+    both[...] = jnp.zeros(both.shape, F32)
+    both[0:3, :] = high.astype(F32)
+    both[3:6, :] = low.astype(F32)
+    for h in range(blocks):
+        tab[48 * h : 48 * h + 48, :] = disp[:, h * WIDE : (h + 1) * WIDE]
+    for h in range(0, blocks, 2):
+        first = both[:, h * WIDE : (h + 1) * WIDE]
+        second = both[:, (h + 1) * WIDE : (h + 2) * WIDE] if h + 1 < blocks else jnp.zeros_like(first)
+        tab[base + 8 * h : base + 8 * h + 16, :] = jnp.concatenate([first, second], 0).astype(BF16)
+    iota = iota_of(WIDE)
+    for p in range(connect.shape[1] // WIDE):
+        ks = slice(p * WIDE, (p + 1) * WIDE)
+        idx = connect[0:1, ks]
+        stacked = jnp.dot(tab[...], one_hot(idx & (WIDE - 1), iota), preferred_element_type=F32)
+        picked[:, ks] = choose(stacked[0:base], idx >> 8, 48).astype(BF16)
+        parts = choose(stacked[base:], idx >> 8, 8)
+        factor[:, ks] = parts + pltpu.roll(parts, 5, 0)
+
+
+def raising(x):
+    largest = jnp.max(jnp.max(jnp.abs(x), axis=1, keepdims=True), axis=0, keepdims=True)
+    largest = jnp.where(largest > 0.0, largest, 1.0)
+    return TOP / largest, largest * (1.0 / TOP)
+
+
+def fill_short(tab, h, block):
+    first = block.astype(SHORT)
+    tab[16 * h : 16 * h + 32, 0:WIDE] = first
+    tab[16 * h : 16 * h + 32, WIDE : 2 * WIDE] = (block - first.astype(F32)).astype(SHORT)
+
+
 def main_kernel(
-    arrived, slot_hbm, weight_hbm, disp_hbm, expansion_hbm, blocks, connect,
+    arrived, slot_hbm, weight_hbm, picked_hbm, factor, blocks, connect,
     prod, near, far,
-    tab, tab3, slot, weight, disp, expansion, matrices, vec, sems,
+    tab, tab3, slot, weight, picked, matrices, heat, vec, sems,
 ):
-    pairs = ((slot_hbm, slot), (weight_hbm, weight), (expansion_hbm, expansion), (disp_hbm, disp), (blocks, matrices))
+    pairs = ((slot_hbm, slot), (weight_hbm, weight), (picked_hbm, picked), (blocks, matrices))
     copies = [pltpu.make_async_copy(source, place, sems.at[i]) for i, (source, place) in enumerate(pairs)]
     for copy in copies:
         copy.start()
     extent = slot.shape[1]
 
+    up, down = raising(jnp.max(jnp.abs(arrived[...]), axis=0))
     for h in range(0, arrived.shape[0] // 2, 2):
-        tiles = [swap_blocks(arrived[2 * h + i]) for i in range(4)]
-        fill_pair(tab, h, jnp.concatenate(tiles[0:2], 1), jnp.concatenate(tiles[2:4], 1))
+        tiles = [swap_blocks(arrived[2 * h + i]) * up for i in range(4)]
+        fill_short(tab, h, jnp.concatenate([jnp.concatenate(tiles[0:2], 1), jnp.concatenate(tiles[2:4], 1)], 0))
     iota = iota_of(WIDE)
-    for copy in copies[0:4]:
+    for copy in copies[0:2]:
         copy.wait()
 
     for j in range(extent // WIDE):
@@ -123,14 +169,22 @@
         for c in range(4):
             idx = slot[c : c + 1, js]
             hot = one_hot(idx & (WIDE - 1), iota)
-            temp = temp + weight[c : c + 1, js] * look_up(tab, hot, idx >> 8)
-        strain = temp / jnp.sqrt(1.0 + temp * temp)
-        for a in range(3):
-            d = disp[16 * a : 16 * a + 16, js].astype(F32)
-            s = (d - expansion[a : a + 1, js] * strain).astype(BF16)
-            tab3[j * 48 + a * 16 : j * 48 + a * 16 + 16, :] = s
-
-    copies[4].wait()
+            hot = hot.astype(SHORT)
+            stacked = jnp.dot(tab[...], jnp.concatenate([hot, hot], 0), preferred_element_type=F32)
+            temp = temp + weight[c : c + 1, js] * choose(stacked, idx >> 8, 16)
+        temp = temp * down
+        heat[:, js] = temp / jnp.sqrt(1.0 + temp * temp)
+
+    up, down = raising(heat[...])
+    for h in range(0, extent // WIDE, 2):
+        first = heat[:, h * WIDE : (h + 1) * WIDE] * up
+        second = jnp.zeros_like(first)
+        if h + 1 < extent // WIDE:
+            second = heat[:, (h + 1) * WIDE : (h + 2) * WIDE] * up
+        fill_short(tab3, h, jnp.concatenate([first, second], 0))
+
+    copies[2].wait()
+    copies[3].wait()
     lane = lax.broadcasted_iota(I32, (16, LANES), 1) >> 5
     count = connect.shape[1] // WIDE
 
@@ -139,8 +193,14 @@
 
     def gather(p):
         idx = indices(p)
-        hot = one_hot(idx & (WIDE - 1), iota)
-        return choose(jnp.dot(tab3[...], hot, preferred_element_type=F32), idx >> 8, 48)
+        hot = one_hot(idx & (WIDE - 1), iota).astype(SHORT)
+        stacked = jnp.dot(tab3[...], jnp.concatenate([hot, hot], 0), preferred_element_type=F32)
+        strain = choose(stacked, idx >> 8, 16) * down
+        ks = slice(p * WIDE, (p + 1) * WIDE)
+        shifted = [
+            picked[16 * a : 16 * a + 16, ks].astype(F32) - factor[a : a + 1, ks] * strain for a in range(3)
+        ]
+        return jnp.concatenate(shifted, 0).astype(BF16).astype(F32)
 
     def multiply(p, got):
         pieces = []
@@ -227,9 +287,14 @@
         out[:, h * WIDE : (h + 1) * WIDE] = first[rows] + second[rows] * (1.0 / RAISE)
 
 
-def ghost_kernel(own, near, far, at, out):
+def ghost_kernel(far, near, own, at_lower, at_upper, out):
+    col = lax.axis_index("col")
+    even = lax.rem(col, 2) == 0
+    edge = (col == 0) | (col == lax.axis_size("col") - 1)
+    at_near = jnp.where(even, at_upper[...], at_lower[...])
+    at_far = jnp.where(edge, -1, jnp.where(even, at_lower[...], at_upper[...]))
     blocks = out.shape[1] // WIDE
-    total = spread(jnp.concatenate([near[...], far[...]], 1), at[...], blocks)
+    total = spread(jnp.concatenate([near[...], far[...]], 1), jnp.concatenate([at_near, at_far], 1), blocks)
     for h in range(blocks):
         hs = slice(h * WIDE, (h + 1) * WIDE)
         out[:, hs] = own[:, hs] + total[48 * h : 48 * h + 48]
@@ -267,40 +332,45 @@
     arrived = arrived.reshape(32, 16, LANES)
     links = connect.T.reshape(1, 4096)
     blocks = jnp.transpose(tangent, (2, 1, 0))
-    col = lax.axis_index("col")
-    even = col % 2 == 0
-    edge = (col == 0) | (col == lax.axis_size("col") - 1)
-    at = jnp.concatenate(
-        [
-            jnp.where(even, recv_upper, recv_lower),
-            jnp.where(edge, -1, jnp.where(even, recv_lower, recv_upper)),
-        ]
-    ).reshape(1, WIDE)
+    picked, factor = pl.pallas_call(
+        pick_kernel,
+        out_shape=(pltpu.HBM((48, 4096), BF16), shape((8, 4096), F32)),
+        in_specs=[away, away, here],
+        out_specs=(here, here),
+        scratch_shapes=[
+            pltpu.VMEM((48, 4352), BF16),
+            pltpu.VMEM((3, 4352), F32),
+            pltpu.VMEM((8, 4352), F32),
+            pltpu.VMEM((17 * 48 + 18 * 8, WIDE), BF16),
+            pltpu.SemaphoreType.DMA((2,)),
+        ],
+        compiler_params=params,
+    )(keep(disp.reshape(48, -1)), keep(expansion), links)
     prod, near, far = pl.pallas_call(
         main_kernel,
         out_shape=(shape((48, 4096), F32), shape((48, LANES), F32), shape((48, LANES), F32)),
-        in_specs=[here, away, away, away, away, free, here],
+        in_specs=[here, away, away, away, here, free, here],
         out_specs=(here, here, here),
         scratch_shapes=[
-            pltpu.VMEM((384, WIDE), BF16),
-            pltpu.VMEM((17 * 48, WIDE), BF16),
+            pltpu.VMEM((256, 2 * WIDE), SHORT),
+            pltpu.VMEM((18 * 16, 2 * WIDE), SHORT),
             pltpu.VMEM((4, 4352), I32),
             pltpu.VMEM((4, 4352), F32),
-            pltpu.VMEM((48, 4352), BF16),
-            pltpu.VMEM((3, 4352), F32),
+            pltpu.VMEM((48, 4096), BF16),
             pltpu.VMEM((128, 96, 96), BF16),
+            pltpu.VMEM((16, 4352), F32),
             pltpu.VMEM((48, 4096), F32),
-            pltpu.SemaphoreType.DMA((5,)),
+            pltpu.SemaphoreType.DMA((4,)),
         ],
         compiler_params=params,
     )(
-        arrived, keep(interp_slot), keep(interp_weight), keep(disp.reshape(48, -1)), keep(expansion), blocks, links
+        arrived, keep(interp_slot), keep(interp_weight), keep(picked), factor, blocks, links
     )
     got_far = swap(far, 1)
     got_near = swap(near, 0)
     own = pl.pallas_call(owned_kernel, out_shape=shape((48, 4096), F32), compiler_params=params)(prod, links)
     result = pl.pallas_call(ghost_kernel, out_shape=shape((48, 4096), F32), compiler_params=params)(
-        own, got_near, got_far, at
+        got_far, got_near, own, recv_lower.reshape(1, LANES), recv_upper.reshape(1, LANES)
     )
     return result.reshape(3, 16, 4096)
 

time: 43.2 us -> 39.8 us (0.921)
  waiting for transfers between devices: 7.89 us -> 2.54 us
  Pallas kernels: 15.7 us -> 16.8 us
  local copies, waits for them, and re-layouts: 4.39 us -> 5.1 us
    all_to_all x1, waiting for transfers between devices: 6.04 us -> 1.42 us  [shards(): lax.all_to_all(packed.reshape(128, 4, LANES), AXES, split_axis=0, concat_...]
    pallas_call x0 -> x1, Pallas kernels: none -> 3.97 us  [shards(): pl.pallas_call(pick_kernel, out_shape=(pltpu.HBM((48, 4096), BF16), shape...]
    pallas_call x1, Pallas kernels: 8.88 us -> 6.05 us  [shards(): pl.pallas_call(main_kernel, out_shape=(shape((48, 4096), F32), shape((48,...]
    ppermute x2, waiting for transfers between devices: 1.85 us -> 1.12 us  [swap(): return lax.ppermute(block, 'col', list(enumerate(partner)))]
    transpose x1, local copies, waits for them, and re-layouts: 0.1 us -> 0.82 us  [shards(): links = connect.T.reshape(1, 4096)]
    unnamed x7 -> x5, local copies, waits for them, and re-layouts: 4.2 us -> 4.19 us
  transfers between devices with their start and end apart: 3 -> 3, of which waited for: 2 -> 3; matrix products, arithmetic and copies ran while one was open for 10% -> 13% of each run, Pallas kernels for 6% -> 17%
where the time goes in v8:
time: 39.8 us; the launch traced here: 39.2 us
  Pallas kernels  16.8 us (42%)
  starting transfers between devices  14.6 us (37%)
  local copies, waits for them, and re-layouts  5.1 us (13%)
  waiting for transfers between devices  2.54 us (6%)
    all_to_all x1, starting transfers between devices, shards(): lax.all_to_all(packed.reshape(128, 4, LANES), AXES, split_axis=0, concat_...  10.5 us
    pallas_call x1, Pallas kernels, shards(): pl.pallas_call(main_kernel, out_shape=(shape((48, 4096), F32), shape((48,...  6.05 us
    unnamed x5, local copies, waits for them, and re-layouts  4.19 us
    ppermute x2, starting transfers between devices, swap(): return lax.ppermute(block, 'col', list(enumerate(partner)))  4.1 us
    pallas_call x1, Pallas kernels, shards(): pl.pallas_call(pick_kernel, out_shape=(pltpu.HBM((48, 4096), BF16), shape...  3.97 us
    pallas_call x1, Pallas kernels, shards(): pl.pallas_call(send_kernel, out_shape=shape((32, 16, LANES), F32), in_spe...  2.83 us
    pallas_call x1, Pallas kernels, shards(): pl.pallas_call(owned_kernel, out_shape=shape((48, 4096), F32), compiler_p...  2.69 us
    all_to_all x1, waiting for transfers between devices, shards(): lax.all_to_all(packed.reshape(128, 4, LANES), AXES, split_axis=0, concat_...  1.42 us
  transfers between devices with their start and end apart: 3, of which 3 were waited for; matrix products, arithmetic and copies ran while one was open for 13% of the time, Pallas kernels for 17%

profile of v8, /device:TPU:2, one launch (start us, length us, event | category | flops | bytes accessed | tf_op | source)
XLA Modules:
  0.0 39.2 jit_solution(11490888622026350576)
XLA Ops:
  0.0 2.8 %shard_map.100 = f32[32,16,128]{2,1,0:T(8,128)} custom-call(f32[16,4096]{1,0:T(8,128)} %temp_hbm.1, s32[1,4096]{1,0:T(1,128)} %index_hbm.1), custom_call_target="tpu_custom_call" | custom-call | tf_op jit(solution)/shard_map/pallas_call | solution.py:318
  2.8 10.5 %all-to-all-start = ((f32[128,4,128]{2,1,0:T(4,128)}), f32[128,4,128]{2,1,0:T(4,128)S(1)}, u32[]{:S(2)}, u32[]{:S(2)}) async-start(f32[128,4,128]{2,1,0:T(4,128)} %bitcast), calls=%async_computation | async-start | bytes 524288 | tf_op jit(solution)/shard_map/all_to_all | solution.py:331
  13.4 0.8 %copy.13 = s32[128,32]{1,0:T(8,128)S(1)} copy(s32[128,32]{0,1:T(8,128)} %bitcast.13) | data formatting | bytes 32768 | tf_op jit(solution)/shard_map/transpose | solution.py:333
  14.2 0.1 reshape.24.connect
  14.3 4.2 %copy.14 = bf16[96,96,128]{0,1,2:T(8,128)(2,1)S(1)} copy(bf16[96,96,128]{2,1,0:T(8,128)(2,1)} %param.16) | data formatting | bytes 4718592 | tf_op args[6]
  18.5 4.0 %shard_map.101 = (bf16[48,4096]{1,0:T(8,128)(2,1)}, f32[8,4096]{1,0:T(8,128)S(1)}) custom-call(bf16[48,4352]{1,0:T(8,128)(2,1)} %bitcast.12, f32[3,4352]{1,0:T(4,128)} %expansion_hbm.1, s32[1,4096]{1,0:T(1,128)S(1)} %reshape.24.connect), custom_call_target="tpu_custom_call" | custom-call | tf_op jit(solution)/shard_map/pallas_call | solution.py:335
  22.5 1.4 %all-to-all-done = f32[128,4,128]{2,1,0:T(4,128)S(1)} async-done(((f32[128,4,128]{2,1,0:T(4,128)}), f32[128,4,128]{2,1,0:T(4,128)S(1)}, u32[]{:S(2)}, u32[]{:S(2)}) %all-to-all-start) | async-done | bytes 262176 | tf_op jit(solution)/shard_map/all_to_all | solution.py:331
  23.9 0.0 copy-start
  23.9 0.0 copy-start.1
  23.9 6.0 %shard_map.102 = (f32[48,4096]{1,0:T(8,128)S(1)}, f32[48,128]{1,0:T(8,128)S(1)}, f32[48,128]{1,0:T(8,128)S(1)}) custom-call(f32[32,16,128]{2,1,0:T(8,128)S(1)} %bitcast.9, s32[4,4352]{1,0:T(4,128)} %slot_hbm.1, f32[4,4352]{1,0:T(4,128)} %weight_hbm.1, bf16[48,4096]{1,0:T(8,128)(2,1)} %get-tuple-element.10.picked_hbm, ...), custom_call_target="tpu_custom_call" | custom-call | tf_op jit(solution)/shard_map/pallas_call | solution.py:349
  29.9 3.8 %collective-permute-start = (f32[48,128]{1,0:T(8,128)S(1)}, f32[48,128]{1,0:T(8,128)S(1)}, u32[]{:S(2)}, u32[]{:S(2)}) collective-permute-start(f32[48,128]{1,0:T(8,128)S(1)} %get-tuple-element.12), channel_id=1, source_target_pairs={{0,0},{1,2},{2,1},{3,4},{4,3},{5,6},{6,5},{7,8},{8,7},{9,10},{10,9... | collective-permute-start | bytes 73736 | tf_op jit(solution)/shard_map/ppermute | solution.py:308
  33.8 0.3 collective-permute-start.1
  34.1 2.7 %shard_map.103.own = f32[48,4096]{1,0:T(8,128)S(1)} custom-call(f32[48,4096]{1,0:T(8,128)S(1)} %get-tuple-element.14.prod, s32[1,4096]{1,0:T(1,128)S(1)} %reshape.24.connect), custom_call_target="tpu_custom_call" | custom-call | tf_op jit(solution)/shard_map/pallas_call | solution.py:371
  36.7 1.0 %collective-permute-done.far = f32[48,128]{1,0:T(8,128)S(1)} collective-permute-done((f32[48,128]{1,0:T(8,128)S(1)}, f32[48,128]{1,0:T(8,128)S(1)}, u32[]{:S(2)}, u32[]{:S(2)}) %collective-permute-start) | collective-permute-done | bytes 24608 | tf_op jit(solution)/shard_map/ppermute | solution.py:308
  37.8 0.1 collective-permute-done.1.near
  37.9 0.0 copy-done
  37.9 0.0 copy-done.1
  37.9 1.3 %shard_map.104 = f32[48,4096]{1,0:T(8,128)} custom-call(f32[48,128]{1,0:T(8,128)S(1)} %collective-permute-done.far, f32[48,128]{1,0:T(8,128)S(1)} %collective-permute-done.1.near, f32[48,4096]{1,0:T(8,128)S(1)} %shard_map.103.own, s32[1,128]{1,0:T(1,128)S(1)} %bitcast.10, s32[1,128]{1,0:T(1,128)S(1)} %bitcast.11), custom_call_target="tpu_custom_call" | custom-call | tf_op jit(solution)/shard_map/pallas_call | solution.py:372
Async XLA Ops:
  2.8 21.0 %all-to-all-start = ((f32[128,4,128]{2,1,0:T(4,128)}), f32[128,4,128]{2,1,0:T(4,128)S(1)}, u32[]{:S(2)}, u32[]{:S(2)}) async-start(f32[128,4,128]{2,1,0:T(4,128)} %bitcast), calls=%async_computation | async-start | bytes 524288 | tf_op jit(solution)/shard_map/all_to_all | solution.py:331
  23.9 14.0 %copy-start = (s32[128]{0:T(128)S(1)}, s32[128]{0:T(128)}, u32[]{:S(2)}) copy-start(s32[128]{0:T(128)} %param.18) | copy-start | bytes 1540
  23.9 14.0 %copy-start.1 = (s32[128]{0:T(128)S(1)}, s32[128]{0:T(128)}, u32[]{:S(2)}) copy-start(s32[128]{0:T(128)} %param.19) | copy-start | bytes 1540
  29.9 7.8 %collective-permute-start = (f32[48,128]{1,0:T(8,128)S(1)}, f32[48,128]{1,0:T(8,128)S(1)}, u32[]{:S(2)}, u32[]{:S(2)}) collective-permute-start(f32[48,128]{1,0:T(8,128)S(1)} %get-tuple-element.12), channel_id=1, source_target_pairs={{0,0},{1,2},{2,1},{3,4},{4,3},{5,6},{6,5},{7,8},{8,7},{9,10},{10,9... | collective-permute-start | bytes 73736 | tf_op jit(solution)/shard_map/ppermute | solution.py:308
  33.8 4.1 %collective-permute-start.1 = (f32[48,128]{1,0:T(8,128)S(1)}, f32[48,128]{1,0:T(8,128)S(1)}, u32[]{:S(2)}, u32[]{:S(2)}) collective-permute-start(f32[48,128]{1,0:T(8,128)S(1)} %get-tuple-element.13), channel_id=1, source_target_pairs={{0,1},{1,0},{2,3},{3,2},{4,5},{5,4},{6,7},{7,6},{8,9},{9,8},{10,11... | collective-permute-start | bytes 73736 | tf_op jit(solution)/shard_map/ppermute | solution.py:308

commit v9 on v8

--- a/solution.py
+++ b/solution.py
@@ -101,7 +101,7 @@
         out[2 * j + 1] = swap_blocks(got[:, LANES:])
 
 
-def pick_kernel(disp_hbm, expansion_hbm, connect, picked, factor, disp, expansion, both, tab, sems):
+def pick_kernel(disp_hbm, expansion_hbm, connect, picked_hbm, factor, disp, expansion, both, tab, picked, sems):
     copies = [
         pltpu.make_async_copy(disp_hbm, disp, sems.at[0]),
         pltpu.make_async_copy(expansion_hbm, expansion, sems.at[1]),
@@ -130,6 +130,12 @@
         picked[:, ks] = choose(stacked[0:base], idx >> 8, 48).astype(BF16)
         parts = choose(stacked[base:], idx >> 8, 8)
         factor[:, ks] = parts + pltpu.roll(parts, 5, 0)
+        if p % 4 == 3:
+            done = pl.ds((p - 3) * WIDE, 4 * WIDE)
+            copies.append(pltpu.make_async_copy(picked.at[:, done], picked_hbm.at[:, done], sems.at[2 + p // 4]))
+            copies[-1].start()
+    for copy in copies[2:]:
+        copy.wait()
 
 
 def raising(x):
@@ -336,13 +342,14 @@
         pick_kernel,
         out_shape=(pltpu.HBM((48, 4096), BF16), shape((8, 4096), F32)),
         in_specs=[away, away, here],
-        out_specs=(here, here),
+        out_specs=(away, here),
         scratch_shapes=[
             pltpu.VMEM((48, 4352), BF16),
             pltpu.VMEM((3, 4352), F32),
             pltpu.VMEM((8, 4352), F32),
             pltpu.VMEM((17 * 48 + 18 * 8, WIDE), BF16),
-            pltpu.SemaphoreType.DMA((2,)),
+            pltpu.VMEM((48, 4096), BF16),
+            pltpu.SemaphoreType.DMA((6,)),
         ],
         compiler_params=params,
     )(keep(disp.reshape(48, -1)), keep(expansion), links)

time: 39.8 us -> 39.7 us (level)
  transfers between devices with their start and end apart: 3 -> 3, of which waited for: 3 -> 2; matrix products, arithmetic and copies ran while one was open for 13% -> 13% of each run, Pallas kernels for 17% -> 17%
where the time goes in v9:
time: 39.7 us; the launch traced here: 39.1 us
  Pallas kernels  16.8 us (42%)
  starting transfers between devices  14.5 us (37%)
  local copies, waits for them, and re-layouts  5.1 us (13%)
  waiting for transfers between devices  2.61 us (7%)
    all_to_all x1, starting transfers between devices, shards(): lax.all_to_all(packed.reshape(128, 4, LANES), AXES, split_axis=0, concat_...  10.5 us
    pallas_call x1, Pallas kernels, shards(): pl.pallas_call(main_kernel, out_shape=(shape((48, 4096), F32), shape((48,...  6.05 us
    unnamed x5, local copies, waits for them, and re-layouts  4.19 us
    ppermute x2, starting transfers between devices, swap(): return lax.ppermute(block, 'col', list(enumerate(partner)))  4.03 us
    pallas_call x1, Pallas kernels, shards(): pl.pallas_call(pick_kernel, out_shape=(pltpu.HBM((48, 4096), BF16), shape...  3.9 us
    pallas_call x1, Pallas kernels, shards(): pl.pallas_call(send_kernel, out_shape=shape((32, 16, LANES), F32), in_spe...  2.83 us
    pallas_call x1, Pallas kernels, shards(): pl.pallas_call(owned_kernel, out_shape=shape((48, 4096), F32), compiler_p...  2.69 us
    all_to_all x1, waiting for transfers between devices, shards(): lax.all_to_all(packed.reshape(128, 4, LANES), AXES, split_axis=0, concat_...  1.49 us
  transfers between devices with their start and end apart: 3, of which 2 were waited for; matrix products, arithmetic and copies ran while one was open for 13% of the time, Pallas kernels for 17%

profile of v9, /device:TPU:2, one launch (start us, length us, event | category | flops | bytes accessed | tf_op | source)
XLA Modules:
  0.0 39.1 jit_solution(12841322209687743539)
XLA Ops:
  0.0 2.8 %shard_map.100 = f32[32,16,128]{2,1,0:T(8,128)} custom-call(f32[16,4096]{1,0:T(8,128)} %temp_hbm.1, s32[1,4096]{1,0:T(1,128)} %index_hbm.1), custom_call_target="tpu_custom_call" | custom-call | tf_op jit(solution)/shard_map/pallas_call | solution.py:324
  2.8 10.5 %all-to-all-start = ((f32[128,4,128]{2,1,0:T(4,128)}), f32[128,4,128]{2,1,0:T(4,128)S(1)}, u32[]{:S(2)}, u32[]{:S(2)}) async-start(f32[128,4,128]{2,1,0:T(4,128)} %bitcast), calls=%async_computation | async-start | bytes 524288 | tf_op jit(solution)/shard_map/all_to_all | solution.py:337
  13.4 0.8 %copy.13 = s32[128,32]{1,0:T(8,128)S(1)} copy(s32[128,32]{0,1:T(8,128)} %bitcast.13) | data formatting | bytes 32768 | tf_op jit(solution)/shard_map/transpose | solution.py:339
  14.2 0.1 reshape.24.connect
  14.3 4.2 %copy.14 = bf16[96,96,128]{0,1,2:T(8,128)(2,1)S(1)} copy(bf16[96,96,128]{2,1,0:T(8,128)(2,1)} %param.16) | data formatting | bytes 4718592 | tf_op args[6]
  18.5 3.9 %shard_map.101 = (bf16[48,4096]{1,0:T(8,128)(2,1)}, f32[8,4096]{1,0:T(8,128)S(1)}) custom-call(bf16[48,4352]{1,0:T(8,128)(2,1)} %bitcast.12, f32[3,4352]{1,0:T(4,128)} %expansion_hbm.1, s32[1,4096]{1,0:T(1,128)S(1)} %reshape.24.connect), custom_call_target="tpu_custom_call" | custom-call | tf_op jit(solution)/shard_map/pallas_call | solution.py:341
  22.4 1.5 %all-to-all-done = f32[128,4,128]{2,1,0:T(4,128)S(1)} async-done(((f32[128,4,128]{2,1,0:T(4,128)}), f32[128,4,128]{2,1,0:T(4,128)S(1)}, u32[]{:S(2)}, u32[]{:S(2)}) %all-to-all-start) | async-done | bytes 262176 | tf_op jit(solution)/shard_map/all_to_all | solution.py:337
  23.9 0.0 copy-start
  23.9 0.0 copy-start.1
  23.9 6.0 %shard_map.102 = (f32[48,4096]{1,0:T(8,128)S(1)}, f32[48,128]{1,0:T(8,128)S(1)}, f32[48,128]{1,0:T(8,128)S(1)}) custom-call(f32[32,16,128]{2,1,0:T(8,128)S(1)} %bitcast.9, s32[4,4352]{1,0:T(4,128)} %slot_hbm.1, f32[4,4352]{1,0:T(4,128)} %weight_hbm.1, bf16[48,4096]{1,0:T(8,128)(2,1)} %get-tuple-element.10.picked_hbm, ...), custom_call_target="tpu_custom_call" | custom-call | tf_op jit(solution)/shard_map/pallas_call | solution.py:356
  29.9 3.8 %collective-permute-start = (f32[48,128]{1,0:T(8,128)S(1)}, f32[48,128]{1,0:T(8,128)S(1)}, u32[]{:S(2)}, u32[]{:S(2)}) collective-permute-start(f32[48,128]{1,0:T(8,128)S(1)} %get-tuple-element.12), channel_id=1, source_target_pairs={{0,0},{1,2},{2,1},{3,4},{4,3},{5,6},{6,5},{7,8},{8,7},{9,10},{10,9... | collective-permute-start | bytes 73736 | tf_op jit(solution)/shard_map/ppermute | solution.py:314
  33.7 0.3 collective-permute-start.1
  34.0 2.7 %shard_map.103.own = f32[48,4096]{1,0:T(8,128)S(1)} custom-call(f32[48,4096]{1,0:T(8,128)S(1)} %get-tuple-element.14.prod, s32[1,4096]{1,0:T(1,128)S(1)} %reshape.24.connect), custom_call_target="tpu_custom_call" | custom-call | tf_op jit(solution)/shard_map/pallas_call | solution.py:378
  36.7 1.1 %collective-permute-done.far = f32[48,128]{1,0:T(8,128)S(1)} collective-permute-done((f32[48,128]{1,0:T(8,128)S(1)}, f32[48,128]{1,0:T(8,128)S(1)}, u32[]{:S(2)}, u32[]{:S(2)}) %collective-permute-start) | collective-permute-done | bytes 24608 | tf_op jit(solution)/shard_map/ppermute | solution.py:314
  37.8 0.0 collective-permute-done.1.near
  37.8 0.0 copy-done
  37.8 0.0 copy-done.1
  37.8 1.3 %shard_map.104 = f32[48,4096]{1,0:T(8,128)} custom-call(f32[48,128]{1,0:T(8,128)S(1)} %collective-permute-done.far, f32[48,128]{1,0:T(8,128)S(1)} %collective-permute-done.1.near, f32[48,4096]{1,0:T(8,128)S(1)} %shard_map.103.own, s32[1,128]{1,0:T(1,128)S(1)} %bitcast.10, s32[1,128]{1,0:T(1,128)S(1)} %bitcast.11), custom_call_target="tpu_custom_call" | custom-call | tf_op jit(solution)/shard_map/pallas_call | solution.py:379
Async XLA Ops:
  2.8 21.0 %all-to-all-start = ((f32[128,4,128]{2,1,0:T(4,128)}), f32[128,4,128]{2,1,0:T(4,128)S(1)}, u32[]{:S(2)}, u32[]{:S(2)}) async-start(f32[128,4,128]{2,1,0:T(4,128)} %bitcast), calls=%async_computation | async-start | bytes 524288 | tf_op jit(solution)/shard_map/all_to_all | solution.py:337
  23.9 13.9 %copy-start = (s32[128]{0:T(128)S(1)}, s32[128]{0:T(128)}, u32[]{:S(2)}) copy-start(s32[128]{0:T(128)} %param.18) | copy-start | bytes 1540
  23.9 13.9 %copy-start.1 = (s32[128]{0:T(128)S(1)}, s32[128]{0:T(128)}, u32[]{:S(2)}) copy-start(s32[128]{0:T(128)} %param.19) | copy-start | bytes 1540
  29.9 7.8 %collective-permute-start = (f32[48,128]{1,0:T(8,128)S(1)}, f32[48,128]{1,0:T(8,128)S(1)}, u32[]{:S(2)}, u32[]{:S(2)}) collective-permute-start(f32[48,128]{1,0:T(8,128)S(1)} %get-tuple-element.12), channel_id=1, source_target_pairs={{0,0},{1,2},{2,1},{3,4},{4,3},{5,6},{6,5},{7,8},{8,7},{9,10},{10,9... | collective-permute-start | bytes 73736 | tf_op jit(solution)/shard_map/ppermute | solution.py:314
  33.7 4.1 %collective-permute-start.1 = (f32[48,128]{1,0:T(8,128)S(1)}, f32[48,128]{1,0:T(8,128)S(1)}, u32[]{:S(2)}, u32[]{:S(2)}) collective-permute-start(f32[48,128]{1,0:T(8,128)S(1)} %get-tuple-element.13), channel_id=1, source_target_pairs={{0,1},{1,0},{2,3},{3,2},{4,5},{5,4},{6,7},{7,6},{8,9},{9,8},{10,11... | collective-permute-start | bytes 73736 | tf_op jit(solution)/shard_map/ppermute | solution.py:314
